TPU v7x, 128 devices: a whole 4x4x4 slice. The times are simulated.
128 devices in a mesh: tm: 32 (over x, y, core), space: 2 (over z_hi), clip: 2 (over z_lo).
Axes of the slice: x: 4, y: 4, z: 4 (z_hi: 2, z_lo: 2; z = z_hi * 2 + z_lo), core: 2. Of those that a mesh axis runs over, the one named last changes fastest.
Arguments:
- video: bfloat16 [2, 128, 8, 10240], P('clip', 'tm', 'space'), may hold values from -35 to 35
- conv_first: bfloat16 [1728, 64], replicated, may hold values from -0.15625 to 0.15625
- conv_second: bfloat16 [1728, 64], replicated, may hold values from -0.15625 to 0.15625
- conv_down: bfloat16 [1728, 128], replicated, may hold values from -0.15625 to 0.15625
- down_cotangent: bfloat16 [2, 128, 4, 10240], P('clip', 'tm', 'space'), may hold values from -6 to 6
Outputs:
- down_features: bfloat16 [2, 128, 4, 10240], P('clip', 'tm', 'space')
- grad_video: float32 [2, 128, 8, 10240], P('clip', 'tm', 'space')
- grad_first: float32 [1728, 64], replicated
- grad_second: float32 [1728, 64], replicated
- grad_down: float32 [1728, 128], replicated
All inputs are finite; a program needn't handle non-finite values.
Results may differ from a plain program's by a relative error of at most 0.0082.
Values may be sent and summed in bfloat16 or wider, within the bound.
A program may use at most 128 MiB of HBM per device.

v0:
```python
import math

import jax
import jax.numpy as jnp
from jax import lax
from jax.sharding import PartitionSpec as P

GROUPS = 32


EPSILON = 1e-06
LAYOUT = ("NDHWC", "DHWIO", "NDHWC")


def shifted(shard, axis, by):
    length = lax.axis_size(axis)
    pairs = [(i, i + by) for i in range(length) if 0 <= i + by < length]
    return lax.ppermute(shard, axis, pairs)


def with_halo(shard, sides, width):
    for axis, dim in sides:
        size, length = (lax.axis_size(axis), shard.shape[dim])
        up = [(i, (i + 1) % size) for i in range(size - 1)]
        down = [(j, i) for i, j in up]
        last = lax.slice_in_dim(shard, length - width, length, axis=dim)
        initial = lax.slice_in_dim(shard, 0, width, axis=dim)
        before = lax.ppermute(last, axis, up)
        after = lax.ppermute(initial, axis, down)
        shard = jnp.concatenate([before, shard, after], axis=dim)
    return shard


def swish(values):
    return values * jax.nn.sigmoid(values)


def group_total(values, groups):
    per_channel = jnp.sum(values.reshape(-1, values.shape[-1]), axis=0)
    return per_channel.reshape(groups, -1).sum(axis=1)


def expand_groups(per_group, channels):
    return jnp.repeat(per_group, channels // per_group.shape[0])


def norm_moments(values, count):
    channels = values.shape[-1]
    centre = lax.psum(group_total(values, GROUPS), ("tm", "space")) / count
    deviation = values - expand_groups(centre, channels)
    variance = lax.psum(group_total(deviation * deviation, GROUPS), ("tm", "space")) / count
    return (expand_groups(centre, channels), expand_groups(lax.rsqrt(variance + EPSILON), channels))


def norm_backward(grad_act, normed, inv_scale, count):
    sigma = jax.nn.sigmoid(normed)
    grad_normed = grad_act * sigma * (1.0 + normed * (1.0 - sigma))
    first_sum, second_sum = lax.psum(
        (group_total(grad_normed, GROUPS), group_total(grad_normed * normed, GROUPS)),
        ("tm", "space"),
    )
    channels = normed.shape[-1]
    return inv_scale * (
        grad_normed
        - expand_groups(first_sum / count, channels)
        - normed * expand_groups(second_sum / count, channels)
    )


def widen(source):
    frame_count = source.shape[0]
    cached = shifted(source[frame_count - 2 :], "tm", 1)
    joined = jnp.concatenate([cached, source], axis=0)
    padded = with_halo(joined, (("space", 1),), 1)
    return jnp.pad(padded, ((0, 0), (0, 0), (1, 1), (0, 0)))


def local_conv(extended, weight, stride):
    in_channels = extended.shape[-1]
    kernel = weight.reshape(3, 3, 3, in_channels, -1)
    result = lax.conv_general_dilated(
        extended[None],
        kernel,
        (1, stride, stride),
        "VALID",
        dimension_numbers=LAYOUT,
        preferred_element_type=jnp.float32,
    )
    return result[0]


def weight_grad(extended, grad_out, stride):
    num_frames, num_rows, num_cols, out_channels = grad_out.shape
    flat_grad = grad_out.reshape(-1, out_channels)
    blocks = []
    for step_t in range(3):
        for step_r in range(3):
            for step_q in range(3):
                view = extended[
                    step_t : step_t + num_frames,
                    step_r : step_r + stride * num_rows : stride,
                    step_q : step_q + stride * num_cols : stride,
                    :,
                ]
                flat_view = view.reshape(-1, extended.shape[-1])
                blocks.append(
                    lax.dot_general(
                        flat_view,
                        flat_grad,
                        (((0,), (0,)), ((), ())),
                        preferred_element_type=jnp.float32,
                    )
                )
    return jnp.concatenate(blocks, axis=0)


def flipped_kernel(weight):
    in_channels = weight.shape[0] // 27
    kernel = weight.reshape(3, 3, 3, in_channels, -1)
    return jnp.transpose(kernel[::-1, ::-1, ::-1], (0, 1, 2, 4, 3))


def with_future(grad_out):
    upcoming = shifted(grad_out[:2], "tm", -1)
    return jnp.concatenate([grad_out, upcoming], axis=0)


def spread_back(grad_out, weight):
    padded = with_halo(with_future(grad_out), (("space", 1),), 1)
    padded = jnp.pad(padded, ((0, 0), (0, 0), (1, 1), (0, 0)))
    result = lax.conv_general_dilated(
        padded[None],
        flipped_kernel(weight),
        (1, 1, 1),
        "VALID",
        dimension_numbers=LAYOUT,
        preferred_element_type=jnp.float32,
    )
    return result[0]


def down_back(grad_out, weight):
    timed = with_future(grad_out)
    below = shifted(timed[:, :1], "space", -1)
    joined = jnp.concatenate([timed, below], axis=1)
    result = lax.conv_general_dilated(
        joined[None],
        flipped_kernel(weight),
        (1, 1, 1),
        [(0, 0), (1, 0), (1, 2)],
        lhs_dilation=(1, 2, 2),
        dimension_numbers=LAYOUT,
        preferred_element_type=jnp.float32,
    )
    return result[0]


def local(video, conv_first, conv_second, conv_down, down_cotangent):
    channels = conv_first.shape[1]
    out_channels = conv_down.shape[1]
    num_frames = video.shape[1]
    num_rows = video.shape[2]
    num_cols = video.shape[3] // channels
    group_devices = lax.axis_size("tm") * lax.axis_size("space")
    count = float(num_frames * num_rows * num_cols * group_devices * (channels // GROUPS))
    all_cells = float(num_frames * num_rows * num_cols * group_devices * lax.axis_size("clip"))
    inputs = video.reshape(num_frames, num_rows, num_cols, channels)
    inputs_wide = inputs.astype(jnp.float32)
    centre_one, scale_one = norm_moments(inputs_wide, count)
    normed_one = (inputs_wide - centre_one) * scale_one
    act_one = swish(normed_one).astype(jnp.bfloat16)
    ext_one = widen(act_one)
    hidden_one = local_conv(ext_one, conv_first, 1).astype(jnp.bfloat16)
    hidden_wide = hidden_one.astype(jnp.float32)
    centre_two, scale_two = norm_moments(hidden_wide, count)
    normed_two = (hidden_wide - centre_two) * scale_two
    act_two = swish(normed_two).astype(jnp.bfloat16)
    ext_two = widen(act_two)
    branch_out = local_conv(ext_two, conv_second, 1)
    block_out = (inputs_wide + branch_out).astype(jnp.bfloat16)
    cached = shifted(block_out[num_frames - 2 :], "tm", 1)
    joined = jnp.concatenate([cached, block_out], axis=0)
    above = shifted(joined[:, num_rows - 1 :], "space", 1)
    ext_down = jnp.pad(jnp.concatenate([above, joined], axis=1), ((0, 0), (0, 0), (1, 0), (0, 0)))
    down_full = local_conv(ext_down, conv_down, 2).astype(jnp.bfloat16)
    down_features = down_full.reshape(1, num_frames, num_rows // 2, num_cols // 2 * out_channels)
    grad_out = down_cotangent.reshape(num_frames, num_rows // 2, num_cols // 2, out_channels)
    raw_down = weight_grad(ext_down, grad_out, 2)
    grad_block = down_back(grad_out, conv_down)
    block_grad16 = grad_block.astype(jnp.bfloat16)
    raw_second = weight_grad(ext_two, block_grad16, 1)
    grad_act_two = spread_back(block_grad16, conv_second)
    grad_hidden = norm_backward(grad_act_two, normed_two, scale_two, count).astype(jnp.bfloat16)
    raw_first = weight_grad(ext_one, grad_hidden, 1)
    grad_act_one = spread_back(grad_hidden, conv_first)
    grad_input = grad_block + norm_backward(grad_act_one, normed_one, scale_one, count)
    sum_first, sum_second, sum_down = lax.psum(
        (raw_first, raw_second, raw_down), ("tm", "space", "clip")
    )
    factor = 1.0 / math.sqrt(all_cells)
    grad_video = grad_input.reshape(1, num_frames, num_rows, num_cols * channels)
    return (down_features, grad_video, sum_first * factor, sum_second * factor, sum_down * factor)


def solution(mesh):
    in_specs = (P("clip", "tm", "space", None), P(), P(), P(), P("clip", "tm", "space", None))
    out_specs = (P("clip", "tm", "space", None), P("clip", "tm", "space", None), P(), P(), P())
    return jax.shard_map(local, mesh=mesh, in_specs=in_specs, out_specs=out_specs, check_vma=False)
```

profile of v0, /device:TPU:1, one launch (start us, length us, event | category | flops | bytes accessed | tf_op | source)
XLA Modules:
  0.0 1503.4 jit_solution(14461032581858000843)
XLA Ops:
  9.8 167.9 %psum.77 = f32[32]{0:T(128)S(1)} all-reduce(f32[32]{0:T(128)S(1)} %reduce_sum.145), channel_id=1, replica_groups=mesh['tm'=32,'space'=2,'clip'=2] {'tm','space'}, use_global_device_ids=true, to_apply=%region_2.0 | all-reduce | flops 32 | bytes 256 | tf_op jit(solution)/shard_map/psum | solution.py:49
  178.5 162.8 %psum.78 = f32[32]{0:T(128)S(1)} all-reduce(f32[32]{0:T(128)S(1)} %reduce_sum.147), channel_id=1, replica_groups=mesh['tm'=32,'space'=2,'clip'=2] {'tm','space'}, use_global_device_ids=true, to_apply=%region_5.0 | all-reduce | flops 32 | bytes 256 | tf_op jit(solution)/shard_map/psum | solution.py:51
  346.8 5.2 collective-permute-start.8
  358.1 2.9 copy.121
  362.0 6.2 collective-permute-start.1
  376.7 3.0 collective-permute-start.10
  385.7 2.8 fusion.306
  391.1 2.8 pad.22.clone
  394.0 3.6 reshape.387
  399.3 2.8 fusion.64
  402.3 164.0 %psum.79 = f32[32]{0:T(128)S(1)} all-reduce(f32[32]{0:T(128)S(1)} %reduce_sum.149), channel_id=1, replica_groups=mesh['tm'=32,'space'=2,'clip'=2] {'tm','space'}, use_global_device_ids=true, to_apply=%region_8.9 | all-reduce | flops 32 | bytes 256 | tf_op jit(solution)/shard_map/psum | solution.py:49
  568.3 162.8 %psum.80 = f32[32]{0:T(128)S(1)} all-reduce(f32[32]{0:T(128)S(1)} %reduce_sum.151), channel_id=1, replica_groups=mesh['tm'=32,'space'=2,'clip'=2] {'tm','space'}, use_global_device_ids=true, to_apply=%region_11.12 | all-reduce | flops 32 | bytes 256 | tf_op jit(solution)/shard_map/psum | solution.py:51
  731.1 2.8 fusion.89
  734.8 4.3 collective-permute-start.11
  752.6 2.8 pad.30.clone
  755.4 3.6 reshape.423
  760.8 7.5 select_reduce_fusion
  768.7 167.0 %all-reduce.7 = (f32[32]{0:T(128)S(1)}, f32[32]{0:T(128)S(1)}) all-reduce(f32[32]{0:T(128)S(1)} %reduce_sum.155, f32[32]{0:T(128)S(1)} %reduce_sum.153), channel_id=1, replica_groups=mesh['tm'=32,'space'=2,'clip'=2] {'tm','space'}, use_global_device_ids=true, to_apply=%region_17.18 | all-reduce | flops 64 | bytes 512 | tf_op jit(solution)/shard_map/psum | solution.py:58
  968.7 5.7 collective-permute-start.13
  991.7 4.0 collective-permute-start.4
  998.0 5.5 collective-permute-start.14
  1026.4 2.8 fusion.80
  1036.2 5.3 fusion.65
  1044.7 2.8 fusion.305
  1054.5 2.9 fusion.71
  1067.0 163.6 %all-reduce.6 = (f32[32]{0:T(128)S(1)}, f32[32]{0:T(128)S(1)}) all-reduce(f32[32]{0:T(128)S(1)} %reduce_sum.159, f32[32]{0:T(128)S(1)} %reduce_sum.157), channel_id=1, replica_groups=mesh['tm'=32,'space'=2,'clip'=2] {'tm','space'}, use_global_device_ids=true, to_apply=%region_23.24 | all-reduce | flops 64 | bytes 512 | tf_op jit(solution)/shard_map/psum | solution.py:58
  1231.2 3.1 multiply_convert_fusion.1
  1256.5 2.9 slice.399
  1277.6 2.9 slice.407
  1301.2 2.9 slice.416
  1324.9 2.9 slice.425
  1340.1 152.1 %all-reduce.10.cloned.1.call-done = (f32[1728,64]{0,1:T(8,128)}, f32[1728,64]{0,1:T(8,128)}, f32[1728,128]{1,0:T(8,128)}) async-done(((f32[1728,64]{0,1:T(8,128)}, f32[1728,64]{0,1:T(8,128)}, f32[1728,128]{1,0:T(8,128)}), (f32[1728,64]{0,1:T(8,128)}, f32[1728,64]{0,1:T(8,128)}, f32[1728,128]{1,0:T(8,128)})) %all-reduce.10.cloned.1.call-update) | async-done | bytes 1769488 | tf_op jit(solution)/shard_map/psum | solution.py:197
  (456 shorter events, 252.6 us)
Async XLA Ops:
  7.2 362.6 %copy-start = (bf16[1728,128]{1,0:T(8,128)(2,1)S(1)}, bf16[1728,128]{1,0:T(8,128)(2,1)}, u32[]{:S(2)}) copy-start(bf16[1728,128]{1,0:T(8,128)(2,1)} %param.8) | copy-start | bytes 1327108
  7.2 1485.0 %all-reduce.10.cloned.1.call-start = ((), (), s32[]{:S(2)}) async-start(), calls=%async_computation | async-start | bytes 3604480 | tf_op jit(solution)/shard_map/psum | solution.py:197
  9.3 333.9 %copy-start.1 = (f32[4,4,160,64]{3,2,1,0:T(8,128)}, f32[4,4,160,64]{3,2,1,0:T(8,128)S(1)}, u32[]{:S(2)}) copy-start(f32[4,4,160,64]{3,2,1,0:T(8,128)S(1)} %reshape.439) | copy-start | bytes 1966084
  341.5 19.4 %copy-start.83 = (f32[64]{0:T(128)}, f32[64]{0:T(128)S(1)}, u32[]{:S(2)}) copy-start(f32[64]{0:T(128)S(1)} %mul.220) | copy-start | bytes 772
  343.1 8.9 copy-start.14
  344.8 16.3 %collective-permute-start = (bf16[2,4,160,64]{2,3,1,0:T(8,128)(2,1)S(1)}, bf16[2,4,160,64]{2,3,1,0:T(8,128)(2,1)S(1)}, u32[]{:S(2)}, u32[]{:S(2)}) collective-permute-start(bf16[2,4,160,64]{2,3,1,0:T(8,128)(2,1)S(1)} %slice.443), channel_id=1, source_target_pairs={{0,4},{4,8},{8,12},{12,16},{16,20},{20,24},{24,28},{28,32},{32,36}... | collective-permute-start | bytes 491528 | tf_op jit(solution)/shard_map/ppermute | solution.py:18
  346.8 9.3 copy-start.56
  346.8 6.1 collective-permute-start.8
  353.0 16.4 %collective-permute-start.9 = (bf16[6,1,80,128]{3,2,1,0:T(8,128)(2,1)S(1)}, bf16[6,1,80,128]{3,2,1,0:T(8,128)(2,1)S(1)}, u32[]{:S(2)}, u32[]{:S(2)}) collective-permute-start(bf16[6,1,80,128]{3,2,1,0:T(8,128)(2,1)S(1)} %slice.452), channel_id=1, source_target_pairs={{2,0},{3,1},{6,4},{7,5},{10,8},{11,9},{14,12},{15,13},{18,16},{19,... | collective-permute-start | bytes 368648 | tf_op jit(solution)/shard_map/ppermute | solution.py:18
  361.1 370.0 %copy-start.8 = (bf16[2,4,160,64]{2,3,1,0:T(8,128)(2,1)}, bf16[2,4,160,64]{2,3,1,0:T(8,128)(2,1)S(1)}, u32[]{:S(2)}) copy-start(bf16[2,4,160,64]{2,3,1,0:T(8,128)(2,1)S(1)} %collective-permute-done) | copy-start | bytes 491524
  362.0 23.8 %collective-permute-start.1 = (bf16[6,1,160,64]{2,3,1,0:T(8,128)(2,1)}, bf16[6,1,160,64]{2,3,1,0:T(8,128)(2,1)}, u32[]{:S(2)}, u32[]{:S(2)}) collective-permute-start(bf16[6,1,160,64]{2,3,1,0:T(8,128)(2,1)} %get-tuple-element.23), channel_id=1, source_target_pairs={{0,2},{1,3},{4,6},{5,7},{8,10},{9,11},{12,14},{13,15},{16,18},{17,... | collective-permute-start | bytes 368648 | tf_op jit(solution)/shard_map/ppermute | solution.py:28
  368.1 17.6 %collective-permute-start.2 = (bf16[6,1,160,64]{2,3,1,0:T(8,128)(2,1)}, bf16[6,1,160,64]{2,3,1,0:T(8,128)(2,1)}, u32[]{:S(2)}, u32[]{:S(2)}) collective-permute-start(bf16[6,1,160,64]{2,3,1,0:T(8,128)(2,1)} %get-tuple-element.24), channel_id=1, source_target_pairs={{2,0},{3,1},{6,4},{7,5},{10,8},{11,9},{14,12},{15,13},{18,16},{19,... | collective-permute-start | bytes 368648 | tf_op jit(solution)/shard_map/ppermute | solution.py:29
  375.5 650.0 %copy-start.3 = (bf16[4,4,1,160,64]{3,4,1,0,2:T(8,128)(2,1)}, bf16[4,4,1,160,64]{3,4,1,0,2:T(8,128)(2,1)S(1)}, u32[]{:S(2)}) copy-start(bf16[4,4,1,160,64]{3,4,1,0,2:T(8,128)(2,1)S(1)} %copy.240) | copy-start | bytes 983044
  376.7 357.3 %collective-permute-start.10 = (bf16[2,4,160,64]{2,3,1,0:T(8,128)(2,1)}, bf16[2,4,160,64]{2,3,1,0:T(8,128)(2,1)S(1)}, u32[]{:S(2)}, u32[]{:S(2)}) collective-permute-start(bf16[2,4,160,64]{2,3,1,0:T(8,128)(2,1)} %bitcast.19), channel_id=1, source_target_pairs={{4,0},{8,4},{12,8},{16,12},{20,16},{24,20},{28,24},{32,28},{36,32}... | collective-permute-start | bytes 491528 | tf_op jit(solution)/shard_map/ppermute | solution.py:18
  402.1 358.7 %copy-start.5 = (bf16[4,4,8,21,64]{4,2,3,1,0:T(8,128)(2,1)}, bf16[4,4,8,21,64]{4,2,3,1,0:T(8,128)(2,1)S(1)}, u32[]{:S(2)}) copy-start(bf16[4,4,8,21,64]{4,2,3,1,0:T(8,128)(2,1)S(1)} %get-tuple-element.33) | copy-start | bytes 1032196
  734.8 10.3 collective-permute-start.11
  739.0 8.2 collective-permute-start.12
  958.8 4.5 copy-start.22
  961.4 29.3 %collective-permute-start.3 = (bf16[2,4,160,64]{2,3,1,0:T(8,128)(2,1)}, bf16[2,4,160,64]{2,3,1,0:T(8,128)(2,1)}, u32[]{:S(2)}, u32[]{:S(2)}) collective-permute-start(bf16[2,4,160,64]{2,3,1,0:T(8,128)(2,1)} %slice.446), channel_id=1, source_target_pairs={{0,4},{4,8},{8,12},{12,16},{16,20},{20,24},{24,28},{28,32},{32,36}... | collective-permute-start | bytes 491528 | tf_op jit(solution)/shard_map/ppermute | solution.py:18
  966.8 7.7 copy-start.9
  968.7 28.3 %collective-permute-start.13 = (bf16[2,4,160,64]{2,3,1,0:T(8,128)(2,1)}, bf16[2,4,160,64]{2,3,1,0:T(8,128)(2,1)}, u32[]{:S(2)}, u32[]{:S(2)}) collective-permute-start(bf16[2,4,160,64]{2,3,1,0:T(8,128)(2,1)} %slice.460), channel_id=1, source_target_pairs={{4,0},{8,4},{12,8},{16,12},{20,16},{24,20},{28,24},{32,28},{36,32}... | collective-permute-start | bytes 491528 | tf_op jit(solution)/shard_map/ppermute | solution.py:18
  991.7 16.9 %collective-permute-start.4 = (bf16[6,1,160,64]{2,3,1,0:T(8,128)(2,1)S(1)}, bf16[6,1,160,64]{2,3,1,0:T(8,128)(2,1)S(1)}, u32[]{:S(2)}, u32[]{:S(2)}) collective-permute-start(bf16[6,1,160,64]{2,3,1,0:T(8,128)(2,1)S(1)} %get-tuple-element.21), channel_id=1, source_target_pairs={{0,2},{1,3},{4,6},{5,7},{8,10},{9,11},{12,14},{13,15},{16,18},{17,... | collective-permute-start | bytes 368648 | tf_op jit(solution)/shard_map/ppermute | solution.py:28
  995.7 12.9 collective-permute-start.5
  998.0 28.5 %collective-permute-start.14 = (bf16[6,1,160,64]{2,3,1,0:T(8,128)(2,1)S(1)}, bf16[6,1,160,64]{2,3,1,0:T(8,128)(2,1)S(1)}, u32[]{:S(2)}, u32[]{:S(2)}) collective-permute-start(bf16[6,1,160,64]{2,3,1,0:T(8,128)(2,1)S(1)} %get-tuple-element.17), channel_id=1, source_target_pairs={{0,2},{1,3},{4,6},{5,7},{8,10},{9,11},{12,14},{13,15},{16,18},{17,... | collective-permute-start | bytes 368648 | tf_op jit(solution)/shard_map/ppermute | solution.py:28
  1003.5 23.0 %collective-permute-start.15 = (bf16[6,1,160,64]{2,3,1,0:T(8,128)(2,1)S(1)}, bf16[6,1,160,64]{2,3,1,0:T(8,128)(2,1)S(1)}, u32[]{:S(2)}, u32[]{:S(2)}) collective-permute-start(bf16[6,1,160,64]{2,3,1,0:T(8,128)(2,1)S(1)} %get-tuple-element.18), channel_id=1, source_target_pairs={{2,0},{3,1},{6,4},{7,5},{10,8},{11,9},{14,12},{15,13},{18,16},{19,... | collective-permute-start | bytes 368648 | tf_op jit(solution)/shard_map/ppermute | solution.py:29
  1010.5 15.0 copy-start.12
  1059.3 5.4 copy-start.7
  1059.3 5.4 copy-start.84
  1060.0 189.6 %collective-permute-start.6 = (bf16[2,4,160,64]{3,2,1,0:T(8,128)(2,1)}, bf16[2,4,160,64]{3,2,1,0:T(8,128)(2,1)}, u32[]{:S(2)}, u32[]{:S(2)}) collective-permute-start(bf16[2,4,160,64]{3,2,1,0:T(8,128)(2,1)} %slice.449), channel_id=1, source_target_pairs={{0,4},{4,8},{8,12},{12,16},{16,20},{20,24},{24,28},{28,32},{32,36}... | collective-permute-start | bytes 491528 | tf_op jit(solution)/shard_map/ppermute | solution.py:18
  1231.2 4.7 copy-start.4
  1247.4 4.5 copy-start.10
  1250.6 4.4 collective-permute-start.7
  (75 other events, 168.6 us)
Sparse Core Ops, SparseCore 0:
  1339.4 152.7 all-reduce.9
where the time goes:
time: 1510 us; the launch traced here: 1500 us
  blocking collectives  988 us (65%)
  local copies, waits for them, and re-layouts  167 us (11%)
  waiting for transfers between devices  156 us (10%)
  matrix products  88.1 us (6%)
  starting transfers between devices  47.9 us (3%)
  other arithmetic  40.1 us (3%)
  between operations  16.5 us (1%)
    psum x2, blocking collectives, norm_moments(): centre = lax.psum(group_total(values, GROUPS), ('tm', 'space')) / count  332 us
    psum x2, blocking collectives, norm_backward(): lax.psum((group_total(grad_normed, GROUPS), group_total(grad_normed * nor...  331 us
    psum x2, blocking collectives, norm_moments(): lax.psum(group_total(deviation * deviation, GROUPS), ('tm', 'space'))  326 us
    psum x1, waiting for transfers between devices, local(): lax.psum((raw_first, raw_second, raw_down), ('tm', 'space', 'clip'))  152 us
    slice x27, local copies, waits for them, and re-layouts, weight_grad(): extended[step_t:step_t + num_frames, step_r:step_r + stride * num_rows:st...  71.3 us
    dot_general x81, matrix products, weight_grad(): lax.dot_general(flat_view, flat_grad, (((0,), (0,)), ((), ())), preferred...  66.3 us
  transfers between devices with their start and end apart: 17, of which 4 were waited for; matrix products, arithmetic and copies ran while one was open for 8% of the time, Pallas kernels for 0%

commit v1 on v0

v1 whole, which is shorter than its diff:
```python
import functools
import math

import jax
import jax.numpy as jnp
from jax import lax
from jax.experimental import pallas as pl
from jax.experimental.pallas import tpu as pltpu
from jax.sharding import PartitionSpec as P

MESH = pl.DeviceIdType.MESH
F32 = jnp.float32
BF16 = jnp.bfloat16
EPSILON = 1e-06
C = 64
C_OUT = 128
T = 4
R = 4
W = 80
L = 128
TM = 32
LOW = 8
HIGH = 8
WIDE = 16
PIECE_SD = 24
PIECE_F = 8
HALF = 864
CELLS = T * R * W
GROUP_CELLS = CELLS * 64


def low_peer(step):
    tm = lax.axis_index("tm")
    low = lax.rem(tm, LOW)
    return {"tm": tm - low + lax.rem(low + step, LOW)}


def high_peer(step):
    tm, space = lax.axis_index("tm"), lax.axis_index("space")
    place = lax.rem((tm // LOW) * 2 + space + step, HIGH)
    return {"tm": (place // 2) * LOW + lax.rem(tm, LOW), "space": lax.rem(place, 2)}


def wide_place():
    return ((lax.axis_index("tm") // LOW) * 2 + lax.axis_index("space")) * 2 + lax.axis_index("clip")


def wide_peer(step):
    tm = lax.axis_index("tm")
    place = lax.rem(wide_place() + step, WIDE)
    return {
        "tm": (place // 4) * LOW + lax.rem(tm, LOW),
        "space": lax.rem(place // 2, 2),
        "clip": lax.rem(place, 2),
    }


def near(step, across):
    tm, space = lax.axis_index("tm"), lax.axis_index("space")
    device = {}
    if step:
        device["tm"] = lax.rem(tm + step + TM, TM)
    if across:
        device["space"] = 1 - space
    return device


def ends(copies):
    for copy in copies:
        copy.wait()


def begins(copies):
    for copy in copies:
        copy.start()
    return copies


def lanes(shape):
    return lax.broadcasted_iota(jnp.int32, shape, len(shape) - 1)


def over_group(value):
    wide = jnp.broadcast_to(value, (8, L))
    both = wide + pltpu.roll(wide, C, 1)
    even = lax.rem(lanes((8, L)), 2) == 0
    other = jnp.where(even, pltpu.roll(both, L - 1, 1), pltpu.roll(both, 1, 1))
    return (both + other)[0:1]


def put_windows(target, f, r, x):
    turned = pltpu.roll(x, C, 1)
    row = lax.broadcasted_iota(jnp.int32, (W, L), 0)
    left = lanes((W, L)) < C
    above = jnp.where(row == 0, 0.0, pltpu.roll(turned, 1, 0))
    below = jnp.where(row == W - 1, 0.0, pltpu.roll(turned, W - 1, 0))
    target[f, r * W : (r + 1) * W, 0:L] = jnp.where(left, above, turned).astype(BF16)
    target[f, r * W : (r + 1) * W, L : 2 * L] = jnp.where(left, turned, below).astype(BF16)


def conv(windows, weights, t):
    total = None
    for dt in range(3):
        for dr in range(3):
            part = jnp.dot(
                windows[t + dt, dr * W : (dr + R) * W, :],
                weights[dt * 3 + dr],
                preferred_element_type=F32,
            )
            total = part if total is None else total + part
    return total


def transposed(source):
    return source.T.astype(BF16)


def kernel(
    video, cot, w_first, w_second, b_first, b_second, w_down, b_down,
    out_down, out_video, out_first, out_second, out_grad_down,
    v_ext, field, c_ext, c_field, c_win, g_block, g_ext, h_ext, t2_ext, t1, win_first, win_second,
    win_back, b_ext, b_even, b_odd, gt, gtc, st_src, st_buf,
    full_sd, send_sd, recv_sd, sum_sd, recvb_sd, total_sd, gather_sd, all_sd,
    full_f, send_f, recv_f, sum_f, recvb_f, total_f, gather_f, all_f,
    halo_sems, st_sems, wa_sems, wb_sems, wc_sems, wd_sems,
):
    tm, space = lax.axis_index("tm"), lax.axis_index("space")
    low = lax.rem(tm, LOW)
    high = (tm // LOW) * 2 + space
    place = wide_place()
    has_past = jnp.where(tm == 0, 0.0, 1.0).astype(F32)
    has_next = jnp.where(tm == TM - 1, 0.0, 1.0).astype(F32)
    has_above = jnp.where(space == 0, 0.0, 1.0).astype(F32)
    has_below = jnp.where(space == 1, 0.0, 1.0).astype(F32)
    one = jnp.ones((), F32)

    def row_mask(r):
        return has_above if r == 0 else has_below if r == R + 1 else one

    edge = pl.multiple_of((R - (R - 1) * space) * W, W)
    far = pl.multiple_of((R + 1) * space * W, W)

    peers = [low_peer(k) for k in range(1, LOW)] + [wide_peer(k) for k in range(1, WIDE)]
    peers += [near(1, False), near(-1, False), near(1, True), near(-1, True)]
    barrier = pltpu.get_barrier_semaphore()
    for peer in peers:
        pl.semaphore_signal(barrier, inc=1, device_id=peer, device_id_type=MESH)

    def remote(source, target, send, recv, device):
        return pltpu.make_async_remote_copy(
            src_ref=source, dst_ref=target, send_sem=send, recv_sem=recv,
            device_id=device, device_id_type=MESH,
        )

    def halo(slot, source, target, device):
        return remote(source, target, halo_sems.at[0, slot], halo_sems.at[1, slot], device)

    def send_stats(k, stage):
        me, peer, size = (low, low_peer, LOW) if stage == 0 else (high, high_peer, HIGH)
        copies = begins([
            remote(
                st_src.at[k, stage], st_buf.at[k, stage, me],
                st_sems.at[0, k, stage, j], st_sems.at[1, k, stage, j], peer(j),
            )
            for j in range(1, size)
        ])
        st_buf[k, stage, me] = st_src[k, stage]
        return copies

    def join_stats(k, stage, copies, centred):
        ends(copies)
        parts = [st_buf[k, stage, j] for j in range(LOW)]
        total = parts[0]
        for part in parts[1:]:
            total = total + part
        first, second = total[0:1], total[1:2]
        if centred:
            cells = float(CELLS * (1 if stage == 0 else LOW))
            first = first * (1.0 / LOW)
            for part in parts:
                second = second + cells * ((part[0:1] - first) * (part[0:1] - first))
        return first, second

    def put_stats(k, stage, first, second):
        st_src[k, stage] = jnp.zeros((8, L), F32)
        st_src[k, stage, 0:1] = first
        st_src[k, stage, 1:2] = second

    def scale_of(mean, spread):
        centre = over_group(mean) * 0.25
        gap = mean - centre
        variance = over_group(spread + float(GROUP_CELLS) * (gap * gap)) * (1.0 / (4 * GROUP_CELLS))
        return centre, lax.rsqrt(variance + EPSILON)

    def spread_of(mean, read):
        def step(t, total):
            gap = read(t) - mean
            return total + jnp.sum(gap * gap, axis=0, keepdims=True)

        return lax.fori_loop(0, T, step, jnp.zeros((1, L), F32))

    def take_video(t, total):
        for p in range(W):
            field[t, pl.ds(p, R, stride=W), :] = video[0, t, :, p * L : (p + 1) * L].astype(F32)
        value = field[t]
        v_ext[t + 2, W : (R + 1) * W, :] = value.astype(BF16)
        return total + jnp.sum(value, axis=0, keepdims=True)

    mean = lax.fori_loop(0, T, take_video, jnp.zeros((1, L), F32)) * (1.0 / CELLS)
    put_stats(0, 0, mean, spread_of(mean, lambda t: field[t]))
    pl.semaphore_wait(barrier, len(peers))
    stats = send_stats(0, 0)
    own = pl.ds(W, R * W)
    video_halo = begins([
        halo(0, v_ext.at[T : T + 2, own], v_ext.at[0:2, own], near(1, False)),
        halo(1, v_ext.at[2 : T + 2, pl.ds(edge, W)], v_ext.at[2 : T + 2, pl.ds(far, W)], near(0, True)),
        halo(2, v_ext.at[T : T + 2, pl.ds(edge, W)], v_ext.at[0:2, pl.ds(far, W)], near(1, True)),
    ])
    for ref in (v_ext, g_ext, h_ext, t2_ext):
        for f in range(ref.shape[0]):
            ref[f, pl.ds(far, W), :] = jnp.zeros((W, L), ref.dtype)

    @pl.loop(0, T)
    def _(t):
        for p in range(W):
            c_field[t, pl.ds(p, 2, stride=W), :] = cot[0, t, :, p * L : (p + 1) * L].astype(F32)
        c_ext[t, 0 : 2 * W, :] = c_field[t].astype(BF16)

    cot_halo = begins([
        halo(3, c_ext.at[0:2, pl.ds(0, 2 * W)], c_ext.at[T : T + 2, pl.ds(0, 2 * W)], near(-1, False)),
        halo(4, c_ext.at[0:T, pl.ds(0, W)], c_ext.at[0:T, pl.ds(2 * W, W)], near(0, True)),
        halo(5, c_ext.at[0:2, pl.ds(0, W)], c_ext.at[T : T + 2, pl.ds(2 * W, W)], near(-1, True)),
    ])
    for half in range(2):
        both = c_field[2 * half : 2 * half + 2].reshape(4 * W, L)
        gtc[:, half * 4 * W : half * 4 * W + 4 * W] = transposed(both)
    put_stats(0, 1, *join_stats(0, 0, stats, True))
    stats = send_stats(0, 1)
    ends(cot_halo)

    @pl.loop(0, T + 2)
    def _(f):
        late = jnp.where(f >= T, has_next, one)
        for r in range(3):
            value = c_ext[f, r * W : (r + 1) * W, :].astype(F32) * (late * has_below if r == 2 else late)
            row = lax.broadcasted_iota(jnp.int32, (W, L), 0)
            after = jnp.where(row == W - 1, 0.0, pltpu.roll(value, W - 1, 0))
            c_win[f, r * W : (r + 1) * W, 0:L] = value.astype(BF16)
            c_win[f, r * W : (r + 1) * W, L : 2 * L] = after.astype(BF16)

    @pl.loop(0, T)
    def _(t):
        even = odd = None
        for j in range(3):
            here = c_win[t + j, 0 : 2 * W, :]
            below = c_win[t + j, W : 3 * W, :]
            a = jnp.dot(here, b_down[j * 3 + 1], preferred_element_type=F32)
            b = jnp.dot(here, b_down[j * 3], preferred_element_type=F32)
            b = b + jnp.dot(below, b_down[j * 3 + 2], preferred_element_type=F32)
            even, odd = (a, b) if j == 0 else (even + a, odd + b)
        for i in range(2):
            for parity, value in ((0, even), (1, odd)):
                r = 2 * i + parity
                piece = value[i * W : (i + 1) * W]
                g_block[t, r * W : (r + 1) * W, :] = piece
                g_ext[t, (r + 1) * W : (r + 2) * W, :] = piece.astype(BF16)

    grad_halo = begins([
        halo(6, g_ext.at[0:2, own], g_ext.at[T : T + 2, own], near(-1, False)),
        halo(7, g_ext.at[0:T, pl.ds(edge, W)], g_ext.at[0:T, pl.ds(far, W)], near(0, True)),
        halo(8, g_ext.at[0:2, pl.ds(edge, W)], g_ext.at[T : T + 2, pl.ds(far, W)], near(-1, True)),
    ])
    for half in range(2):
        both = g_ext[2 * half : 2 * half + 2, W : (R + 1) * W, :].reshape(8 * W, L)
        gt[:, half * 8 * W : (half + 1) * 8 * W] = transposed(both.astype(F32))

    centre_one, scale_one = scale_of(*join_stats(0, 1, stats, True))
    ends(video_halo)

    @pl.loop(0, T + 2)
    def _(f):
        early = jnp.where(f < 2, has_past, one)
        for r in range(R + 2):
            normed = (v_ext[f, r * W : (r + 1) * W, :].astype(F32) - centre_one) * scale_one
            put_windows(win_first, f, r, normed * jax.nn.sigmoid(normed) * (early * row_mask(r)))

    def first_conv(t, total):
        hidden = conv(win_first, w_first, t).astype(BF16)
        h_ext[t + 2, W : (R + 1) * W, :] = hidden
        return total + jnp.sum(hidden.astype(F32), axis=0, keepdims=True)

    mean = lax.fori_loop(0, T, first_conv, jnp.zeros((1, L), F32)) * (1.0 / CELLS)

    def own_hidden(t):
        return h_ext[t + 2, W : (R + 1) * W, :].astype(F32)

    put_stats(1, 0, mean, spread_of(mean, own_hidden))
    stats = send_stats(1, 0)
    hidden_halo = begins([
        halo(9, h_ext.at[T : T + 2, own], h_ext.at[0:2, own], near(1, False)),
        halo(10, h_ext.at[2 : T + 2, pl.ds(edge, W)], h_ext.at[2 : T + 2, pl.ds(far, W)], near(0, True)),
        halo(11, h_ext.at[T : T + 2, pl.ds(edge, W)], h_ext.at[0:2, pl.ds(far, W)], near(1, True)),
        halo(12, h_ext.at[2:4, own], h_ext.at[T + 2 : T + 4, own], near(-1, False)),
        halo(13, h_ext.at[2:4, pl.ds(edge, W)], h_ext.at[T + 2 : T + 4, pl.ds(far, W)], near(-1, True)),
    ])

    ends(grad_halo)

    @pl.loop(0, T + 2)
    def _(f):
        late = jnp.where(f >= T, has_next, one)
        for r in range(R + 2):
            value = g_ext[f, r * W : (r + 1) * W, :].astype(F32) * (late * row_mask(r))
            put_windows(win_back, f, r, value)

    put_stats(1, 1, *join_stats(1, 0, stats, True))
    stats = send_stats(1, 1)

    @pl.loop(0, T)
    def _(t):
        t2_ext[t, W : (R + 1) * W, :] = conv(win_back, b_second, t)

    act_halo = begins([
        halo(14, t2_ext.at[0:2, own], t2_ext.at[T : T + 2, own], near(-1, False)),
        halo(15, t2_ext.at[0:T, pl.ds(edge, W)], t2_ext.at[0:T, pl.ds(far, W)], near(0, True)),
        halo(16, t2_ext.at[0:2, pl.ds(edge, W)], t2_ext.at[T : T + 2, pl.ds(far, W)], near(-1, True)),
    ])

    centre_two, scale_two = scale_of(*join_stats(1, 1, stats, True))

    def gradient(grad, normed):
        sigma = jax.nn.sigmoid(normed)
        return grad * sigma * (1.0 + normed * (1.0 - sigma))

    def second_sums(t, sums):
        first, second = sums
        for r in range(1, R + 1):
            normed = (h_ext[t + 2, r * W : (r + 1) * W, :].astype(F32) - centre_two) * scale_two
            grad = gradient(t2_ext[t, r * W : (r + 1) * W, :], normed)
            first = first + jnp.sum(grad, axis=0, keepdims=True)
            second = second + jnp.sum(grad * normed, axis=0, keepdims=True)
        return first, second

    nothing = (jnp.zeros((1, L), F32), jnp.zeros((1, L), F32))
    put_stats(2, 0, *lax.fori_loop(0, T, second_sums, nothing))
    stats = send_stats(2, 0)
    ends(hidden_halo)

    @pl.loop(0, T + 2)
    def _(f):
        early = jnp.where(f < 2, has_past, one)
        for r in range(R + 2):
            normed = (h_ext[f, r * W : (r + 1) * W, :].astype(F32) - centre_two) * scale_two
            put_windows(win_second, f, r, normed * jax.nn.sigmoid(normed) * (early * row_mask(r)))

    put_stats(2, 1, *join_stats(2, 0, stats, False))
    stats = send_stats(2, 1)

    @pl.loop(0, T)
    def _(t):
        block = v_ext[t + 2, W : (R + 1) * W, :].astype(F32) + conv(win_second, w_second, t)
        b_ext[t + 2, W : (R + 1) * W, :] = block.astype(BF16)

    block_halo = begins([
        halo(17, b_ext.at[T : T + 2, own], b_ext.at[0:2, own], near(1, False)),
        halo(18, b_ext.at[2 : T + 2, pl.ds(R * W, W)], b_ext.at[2 : T + 2, pl.ds(0, W)], near(0, True)),
        halo(19, b_ext.at[T : T + 2, pl.ds(R * W, W)], b_ext.at[0:2, pl.ds(0, W)], near(1, True)),
    ])

    def block_weights(windows, full, base):
        left = lanes((3 * C, L)) < C

        def folded(dt, dr):
            cells = windows[dt : dt + T, dr * W : (dr + R) * W, :].reshape(CELLS, 2 * L)
            turned = jnp.dot(gt[...], cells, preferred_element_type=F32).T
            return turned[0 : 3 * C] + pltpu.roll(turned[C : 4 * C], C, 1)

        for pair in range(4):
            a, b = 2 * pair, 2 * pair + 1
            value = jnp.where(left, folded(a // 3, a % 3), pltpu.roll(folded(b // 3, b % 3), C, 1))
            full[base + pair * 3 * C : base + (pair + 1) * 3 * C, :] = value
        value = folded(2, 2)
        half = 3 * C // 2
        value = jnp.where(left[0:half], value[0:half], pltpu.roll(value[half:], C, 1))
        full[base + 12 * C : base + 12 * C + half, :] = value

    full_sd[HALF + 27 * C :, :] = jnp.zeros((full_sd.shape[0] - HALF - 27 * C, L), F32)
    full_f[HALF:, :] = jnp.zeros((full_f.shape[0] - HALF, L), F32)
    block_weights(win_second, full_sd, 0)

    ends(block_halo)

    @pl.loop(0, T + 2)
    def _(f):
        early = jnp.where(f < 2, has_past, one)
        for r in range(R + 1):
            value = b_ext[f, r * W : (r + 1) * W, :].astype(F32) * (early * has_above if r == 0 else early)
            put_windows(b_odd if r % 2 else b_even, f, r // 2, value)

    def projected(dr):
        return (b_even, 0) if dr == 0 else (b_odd, 0) if dr == 1 else (b_even, W)

    @pl.loop(0, T)
    def _(t):
        total = None
        for dt in range(3):
            for dr in range(3):
                ref, start = projected(dr)
                part = jnp.dot(
                    ref[t + dt, start : start + 2 * W, 0 : 3 * C],
                    w_down[dt * 3 + dr],
                    preferred_element_type=F32,
                )
                total = part if total is None else total + part
        c_field[t] = total
        for p in range(W):
            out_down[0, t, :, p * L : (p + 1) * L] = c_field[t, pl.ds(p, 2, stride=W), :].astype(BF16)

    for dt in range(3):
        for dr in range(3):
            ref, start = projected(dr)
            cells = ref[dt : dt + T, start : start + 2 * W, :].reshape(2 * W * T, 2 * L)
            turned = jnp.dot(gtc[...], cells, preferred_element_type=F32).T
            base = HALF + (dt * 3 + dr) * 3 * C
            full_sd[base : base + 3 * C, :] = turned[0 : 3 * C]

    def part_of(index, rows):
        return pl.ds(pl.multiple_of(index * rows, 8), rows)

    class Reduction:
        def __init__(self, number, piece, full, send, recv, sums, recvb, total, gather, whole):
            self.n, self.piece, self.rows = number, piece, piece * WIDE
            self.full, self.send, self.recv, self.sums = full, send, recv, sums
            self.recvb, self.total, self.gather, self.whole = recvb, total, gather, whole

        def sem(self, sems, k):
            return sems.at[0, self.n, k], sems.at[1, self.n, k]

        def start(self):
            self.send[...] = self.full[...].astype(BF16)
            self.copies = begins([
                remote(
                    self.send.at[part_of(lax.rem(low + k, LOW), self.rows)], self.recv.at[k - 1],
                    *self.sem(wa_sems, k), low_peer(k),
                )
                for k in range(1, LOW)
            ])

        def second(self):
            ends(self.copies)
            value = self.full[part_of(low, self.rows), :]
            for k in range(LOW - 1):
                value = value + self.recv[k].astype(F32)
            self.sums[...] = value
            self.copies = begins([
                remote(
                    self.sums.at[part_of(lax.rem(place + k, WIDE), self.piece)], self.recvb.at[k - 1],
                    *self.sem(wb_sems, k), wide_peer(k),
                )
                for k in range(1, WIDE)
            ])

        def third(self):
            ends(self.copies)
            value = self.sums[part_of(place, self.piece), :]
            for k in range(WIDE - 1):
                value = value + self.recvb[k]
            value = value * (1.0 / math.sqrt(2 * 128 * 8 * 160))
            self.total[...] = value
            self.copies = begins([
                remote(
                    self.total, self.gather.at[part_of(place, self.piece)],
                    *self.sem(wc_sems, k), wide_peer(k),
                )
                for k in range(1, WIDE)
            ])
            self.gather[part_of(place, self.piece), :] = value

        def fourth(self):
            ends(self.copies)
            here = pl.ds(pl.multiple_of(low * self.rows, 16), self.rows)
            self.whole[here, :] = self.gather[...].astype(BF16)
            self.copies = begins([
                remote(
                    self.whole.at[here], self.whole.at[here], *self.sem(wd_sems, k), low_peer(k),
                )
                for k in range(1, LOW)
            ])

        def finish(self):
            ends(self.copies)

    sums_sd = Reduction(0, PIECE_SD, full_sd, send_sd, recv_sd, sum_sd, recvb_sd, total_sd, gather_sd, all_sd)
    sums_f = Reduction(1, PIECE_F, full_f, send_f, recv_f, sum_f, recvb_f, total_f, gather_f, all_f)
    sums_sd.start()

    count = 1.0 / (4 * GROUP_CELLS)
    ends(act_halo)
    first, second = join_stats(2, 1, stats, False)
    mean_one, mean_two = over_group(first) * count, over_group(second) * count

    @pl.loop(0, T + 2)
    def _(f):
        late = jnp.where(f >= T, has_next, one)
        for r in range(R + 2):
            normed = (h_ext[f + 2, r * W : (r + 1) * W, :].astype(F32) - centre_two) * scale_two
            grad = gradient(t2_ext[f, r * W : (r + 1) * W, :], normed)
            hidden = scale_two * (grad - mean_one - normed * mean_two)
            put_windows(win_back, f, r, hidden * (late * row_mask(r)))
            if 1 <= r <= R:

                @pl.when(f < T)
                def _():
                    field[f, (r - 1) * W : r * W, :] = hidden

    def back_first(t, sums):
        back = conv(win_back, b_first, t)
        normed = (v_ext[t + 2, W : (R + 1) * W, :].astype(F32) - centre_one) * scale_one
        grad = gradient(back, normed)
        t1[t] = grad
        return (
            sums[0] + jnp.sum(grad, axis=0, keepdims=True),
            sums[1] + jnp.sum(grad * normed, axis=0, keepdims=True),
        )

    put_stats(3, 0, *lax.fori_loop(0, T, back_first, nothing))
    stats = send_stats(3, 0)
    sums_sd.second()
    for half in range(2):
        both = field[2 * half : 2 * half + 2].reshape(8 * W, L)
        gt[:, half * 8 * W : (half + 1) * 8 * W] = transposed(both)
    block_weights(win_first, full_f, 0)
    sums_f.start()
    put_stats(3, 1, *join_stats(3, 0, stats, False))
    stats = send_stats(3, 1)
    sums_sd.third()
    sums_f.second()
    first, second = join_stats(3, 1, stats, False)
    mean_one, mean_two = over_group(first) * count, over_group(second) * count
    sums_sd.fourth()

    @pl.loop(0, T)
    def _(t):
        normed = (v_ext[t + 2, W : (R + 1) * W, :].astype(F32) - centre_one) * scale_one
        field[t] = g_block[t] + scale_one * (t1[t] - mean_one - normed * mean_two)
        for p in range(W):
            out_video[0, t, :, p * L : (p + 1) * L] = field[t, pl.ds(p, R, stride=W), :]

    sums_f.third()
    sums_f.fourth()

    def unpack(source, base, target):
        for pair in range(4):
            value = source[base + pair * 3 * C : base + (pair + 1) * 3 * C, :].astype(F32)
            target[pair * 6 * C : pair * 6 * C + 3 * C, :] = value[:, 0:C]
            target[pair * 6 * C + 3 * C : (pair + 1) * 6 * C, :] = pltpu.roll(value, C, 1)[:, 0:C]
        half = 3 * C // 2
        value = source[base + 12 * C : base + 12 * C + half, :].astype(F32)
        target[24 * C : 24 * C + half, :] = value[:, 0:C]
        target[24 * C + half : 27 * C, :] = pltpu.roll(value, C, 1)[:, 0:C]

    sums_sd.finish()
    unpack(all_sd, 0, out_second)
    out_grad_down[...] = all_sd[HALF : HALF + 27 * C, :].astype(F32)
    sums_f.finish()
    unpack(all_f, 0, out_first)


def windowed(kernels):
    flat = kernels.reshape(9, 3 * C, C)
    empty = jnp.zeros((9, C, C), flat.dtype)
    return jnp.concatenate(
        [jnp.concatenate([flat, empty], axis=1), jnp.concatenate([empty, flat], axis=1)], axis=2
    )


def flipped(weight, channels):
    return jnp.swapaxes(weight.reshape(27, C, channels)[::-1], 1, 2)


def local(video, conv_first, conv_second, conv_down, down_cotangent):
    back_down = flipped(conv_down, C_OUT).reshape(9, 3, C_OUT, C)
    upper = jnp.concatenate([back_down[:, 1], back_down[:, 0]], axis=2)
    lower = jnp.concatenate([jnp.zeros_like(back_down[:, 2]), back_down[:, 2]], axis=2)
    operands = (
        video,
        down_cotangent,
        windowed(conv_first.reshape(9, 3, C, C)),
        windowed(conv_second.reshape(9, 3, C, C)),
        windowed(flipped(conv_first, C).reshape(9, 3, C, C)),
        windowed(flipped(conv_second, C).reshape(9, 3, C, C)),
        conv_down.reshape(9, 3 * C, C_OUT),
        jnp.concatenate([upper, lower], axis=1),
    )
    rows = (R + 2) * W

    def reduction(piece):
        total, part = piece * WIDE * LOW, piece * WIDE
        return [
            pltpu.VMEM((total, L), F32),
            pltpu.VMEM((total, L), BF16),
            pltpu.VMEM((LOW - 1, part, L), BF16),
            pltpu.VMEM((part, L), F32),
            pltpu.VMEM((WIDE - 1, piece, L), F32),
            pltpu.VMEM((piece, L), F32),
            pltpu.VMEM((part, L), F32),
            pltpu.VMEM((total, L), BF16),
        ]

    vmem = pl.BlockSpec(memory_space=pltpu.VMEM)
    dma = pltpu.SemaphoreType.DMA
    return pl.pallas_call(
        kernel,
        out_shape=(
            jax.ShapeDtypeStruct((1, T, 2, W * L), BF16),
            jax.ShapeDtypeStruct((1, T, R, W * L), F32),
            jax.ShapeDtypeStruct((27 * C, C), F32),
            jax.ShapeDtypeStruct((27 * C, C), F32),
            jax.ShapeDtypeStruct((27 * C, C_OUT), F32),
        ),
        in_specs=[vmem] * len(operands),
        out_specs=(vmem,) * 5,
        scratch_shapes=[
            pltpu.VMEM((T + 2, rows, L), BF16),
            pltpu.VMEM((T, R * W, L), F32),
            pltpu.VMEM((T + 2, 3 * W, L), BF16),
            pltpu.VMEM((T, 2 * W, L), F32),
            pltpu.VMEM((T + 2, 3 * W, 2 * L), BF16),
            pltpu.VMEM((T, R * W, L), F32),
            pltpu.VMEM((T + 2, rows, L), BF16),
            pltpu.VMEM((T + 4, rows, L), BF16),
            pltpu.VMEM((T + 2, rows, L), F32),
            pltpu.VMEM((T, R * W, L), F32),
            pltpu.VMEM((T + 2, rows, 2 * L), BF16),
            pltpu.VMEM((T + 2, rows, 2 * L), BF16),
            pltpu.VMEM((T + 2, rows, 2 * L), BF16),
            pltpu.VMEM((T + 2, (R + 1) * W, L), BF16),
            pltpu.VMEM((T + 2, 3 * W, 2 * L), BF16),
            pltpu.VMEM((T + 2, 2 * W, 2 * L), BF16),
            pltpu.VMEM((L, CELLS), BF16),
            pltpu.VMEM((L, CELLS // 2), BF16),
            pltpu.VMEM((4, 2, 8, L), F32),
            pltpu.VMEM((4, 2, LOW, 8, L), F32),
            *reduction(PIECE_SD),
            *reduction(PIECE_F),
            dma((2, 20)),
            dma((2, 4, 2, LOW)),
            dma((2, 2, LOW)),
            dma((2, 2, WIDE)),
            dma((2, 2, WIDE)),
            dma((2, 2, LOW)),
        ],
        compiler_params=pltpu.CompilerParams(
            collective_id=1, has_side_effects=True, vmem_limit_bytes=56 * 1024 * 1024
        ),
    )(*operands)


def solution(mesh):
    in_specs = (P("clip", "tm", "space", None), P(), P(), P(), P("clip", "tm", "space", None))
    out_specs = (P("clip", "tm", "space", None), P("clip", "tm", "space", None), P(), P(), P())
    return jax.shard_map(local, mesh=mesh, in_specs=in_specs, out_specs=out_specs, check_vma=False)
```

time: 1510 us -> 105 us (0.07)
  blocking collectives: 988 us -> 0 us
  local copies, waits for them, and re-layouts: 167 us -> 10.7 us
  waiting for transfers between devices: 156 us -> 0 us
  Pallas kernels: 0 us -> 88.9 us
  matrix products: 88.1 us -> 0 us
  starting transfers between devices: 47.9 us -> 0 us
  other arithmetic: 40.1 us -> 4.37 us
  between operations: 16.5 us -> 0.73 us
    psum x6 -> x0, blocking collectives: 988 us -> none  [the longest x2 332 us: norm_moments(): centre = lax.psum(group_total(values, GROUPS), ('tm', 'space')) / count]
    psum x1 -> x0, waiting for transfers between devices: 152 us -> none  [local(): lax.psum((raw_first, raw_second, raw_down), ('tm', 'space', 'clip'))]
    pallas_call x0 -> x1, Pallas kernels: none -> 88.9 us  [local(): pl.pallas_call(kernel, out_shape=(jax.ShapeDtypeStruct((1, T, 2, W * L),...]
    slice x35 -> x1, local copies, waits for them, and re-layouts: 73.6 us -> 0.03 us  [local(): upper = jnp.concatenate([back_down[:, 1], back_down[:, 0]], axis=2)]
    dot_general x81 -> x0, matrix products: 66.3 us -> none  [weight_grad(): lax.dot_general(flat_view, flat_grad, (((0,), (0,)), ((), ())), preferred...]
    ppermute x16 -> x0, starting transfers between devices: 47.9 us -> none  [the longest x8 22.4 us: shifted(): return lax.ppermute(shard, axis, pairs)]
    conv_general_dilated x28 -> x0, local copies, waits for them, and re-layouts: 25.4 us -> none  [the longest x11 12.5 us: spread_back(): lax.conv_general_dilated(padded[None], flipped_kernel(weight), (1, 1, 1),...]
    unnamed x190 -> x20, local copies, waits for them, and re-layouts: 26.6 us -> 3.9 us
  transfers between devices with their start and end apart: 17 -> 0, of which waited for: 4 -> 0; matrix products, arithmetic and copies ran while one was open for 8% -> 0% of each run, Pallas kernels for 0% -> 0%
where the time goes in v1:
time: 105 us
  Pallas kernels  88.9 us (85%)
  local copies, waits for them, and re-layouts  10.7 us (10%)
  other arithmetic  4.37 us (4%)
    pallas_call x1, Pallas kernels, local(): pl.pallas_call(kernel, out_shape=(jax.ShapeDtypeStruct((1, T, 2, W * L),...  88.9 us
    unnamed x20, local copies, waits for them, and re-layouts  3.9 us
    pallas_call x2, local copies, waits for them, and re-layouts, local(): pl.pallas_call(kernel, out_shape=(jax.ShapeDtypeStruct((1, T, 2, W * L),...  3.35 us
    concatenate x2, other arithmetic, windowed(): jnp.concatenate([jnp.concatenate([flat, empty], axis=1), jnp.concatenate(...  2.81 us
    rev x3, local copies, waits for them, and re-layouts, flipped(): return jnp.swapaxes(weight.reshape(27, C, channels)[::-1], 1, 2)  2.1 us

profile of v1, /device:TPU:1, one launch (start us, length us, event | category | flops | bytes accessed | tf_op | source)
XLA Modules:
  0.0 104.8 jit_solution(3290735681555551619)
XLA Ops:
  0.6 1.0 rev.11
  1.7 0.0 copy-start
  1.7 0.2 copy.25
  2.0 0.2 copy.26
  2.2 0.2 copy.27
  2.4 0.2 copy-done
  2.7 0.3 copy.16
  2.9 0.0 copy-start.1
  2.9 1.6 %fusion.9 = (bf16[9,256,128]{2,1,0:T(8,128)(2,1)}, bf16[9,256,128]{2,1,0:T(8,128)(2,1)}) fusion(bf16[9,128,64]{2,1,0:T(8,128)(2,1)S(1)} %bitcast.29, bf16[9,128,64]{2,1,0:T(8,128)(2,1)S(1)} %bitcast.28, bf16[9,128,64]{2,1,0:T(8,128)(2,1)S(1)} %bitcast.27, bf16[9,192,64]{2,1,0:T(8,128)(2,1)S(1)} %bitcast.21), kind=kLoop, calls=%fused_computation.12 | loop fusion | flops 4718592 | bytes 1843200 | tf_op jit(solution)/shard_map/concatenate | solution.py:593
  4.5 0.0 copy-done.1
  4.5 0.3 copy.17
  4.8 0.5 reshape.25
  5.3 0.5 rev.9
  5.8 0.2 copy.18
  6.0 1.7 %fusion.11 = (bf16[9,256,128]{2,1,0:T(8,128)(2,1)}, bf16[9,256,128]{2,1,0:T(8,128)(2,1)}) fusion(bf16[9,192,64]{2,1,0:T(8,128)(2,1)S(1)} %bitcast.25, bf16[9,192,64]{2,1,0:T(8,128)(2,1)S(1)} %bitcast.26), kind=kLoop, calls=%fused_computation.14 | loop fusion | flops 4128768 | bytes 1622016 | tf_op jit(solution)/shard_map/concatenate | solution.py:572
  7.6 0.5 reshape.26
  8.1 0.5 rev.10
  8.7 0.2 copy.19
  8.8 1.2 %fusion.13.b_second = bf16[9,256,128]{2,1,0:T(8,128)(2,1)} fusion(bf16[9,192,64]{2,1,0:T(8,128)(2,1)S(1)} %bitcast.22), kind=kLoop, calls=%fused_computation.16 | loop fusion | flops 2359296 | bytes 811008 | tf_op jit(solution)/shard_map/concatenate | solution.py:572
  10.0 88.9 %shard_map.92 = (bf16[1,4,2,10240]{3,2,1,0:T(2,128)(2,1)}, f32[1,4,4,10240]{3,2,1,0:T(4,128)}, f32[1728,64]{1,0:T(8,128)}, f32[1728,64]{1,0:T(8,128)}, f32[1728,128]{1,0:T(8,128)}) custom-call(bf16[1,4,4,10240]{3,2,1,0:T(4,128)(2,1)} %video.1, bf16[1,4,2,10240]{3,2,1,0:T(2,128)(2,1)} %cot.1, bf16[9,256,128]{2,1,0:T(8,128)(2,1)} %get-tuple-element.19.w_first, ...), custom_call_target="tpu_custom_call" | custom-call | tf_op jit(solution)/shard_map/pallas_call | solution.py:612
  99.0 0.0 copy-start.3
  99.0 2.3 %copy.23 = f32[1728,64]{0,1:T(8,128)} copy(f32[1728,64]{1,0:T(8,128)} %get-tuple-element.12) | data formatting | bytes 884736 | tf_op jit(solution)/shard_map/pallas_call | solution.py:612
  101.3 0.0 copy-done.3
  101.3 0.0 copy-start.5
  101.3 0.0 copy-start.4
  101.3 1.1 %copy.24 = f32[1728,64]{0,1:T(8,128)} copy(f32[1728,64]{1,0:T(8,128)S(1)} %copy-done.3) | data formatting | bytes 884736 | tf_op jit(solution)/shard_map/pallas_call | solution.py:612
  102.3 0.0 copy-done.5
  102.3 0.7 copy.31
  103.0 0.0 copy-done.4
  103.0 0.8 copy.32
  103.8 0.0 copy-done.2
  103.8 0.9 copy.33
  (2 shorter events, 0.0 us)
Async XLA Ops:
  1.7 0.9 copy-start
  2.9 1.6 %copy-start.1 = (bf16[1728,64]{0,1:T(8,128)(2,1)S(1)}, bf16[1728,64]{0,1:T(8,128)(2,1)}, u32[]{:S(2)}) copy-start(bf16[1728,64]{0,1:T(8,128)(2,1)} %param.7) | copy-start | bytes 663556
  99.0 2.3 %copy-start.3 = (f32[1728,64]{1,0:T(8,128)S(1)}, f32[1728,64]{1,0:T(8,128)}, u32[]{:S(2)}) copy-start(f32[1728,64]{1,0:T(8,128)} %get-tuple-element.13) | copy-start | bytes 1327108
  101.3 1.1 %copy-start.5 = (bf16[1,4,2,10240]{3,2,1,0:T(2,128)(2,1)S(1)}, bf16[1,4,2,10240]{3,2,1,0:T(2,128)(2,1)}, u32[]{:S(2)}) copy-start(bf16[1,4,2,10240]{3,2,1,0:T(2,128)(2,1)} %get-tuple-element.27) | copy-start | bytes 491524
  101.3 1.7 %copy-start.4 = (f32[1,4,4,10240]{3,2,1,0:T(4,128)S(1)}, f32[1,4,4,10240]{3,2,1,0:T(4,128)}, u32[]{:S(2)}) copy-start(f32[1,4,4,10240]{3,2,1,0:T(4,128)} %get-tuple-element.28) | copy-start | bytes 1966084
  102.3 1.5 %copy-start.2 = (f32[1728,128]{1,0:T(8,128)S(1)}, f32[1728,128]{1,0:T(8,128)}, u32[]{:S(2)}) copy-start(f32[1728,128]{1,0:T(8,128)} %get-tuple-element.31) | copy-start | bytes 2654212

commit v2 on v1

--- a/solution.py
+++ b/solution.py
@@ -21,10 +21,12 @@
 TM = 32
 LOW = 8
 HIGH = 8
-WIDE = 16
-PIECE_SD = 24
-PIECE_F = 8
-HALF = 864
+PLANE = 16
+COLUMN = 8
+PIECE_SD = 176
+PIECE_F = 64
+TILES = 14
+HALF = TILES * C
 CELLS = T * R * W
 GROUP_CELLS = CELLS * 64
 
@@ -41,15 +43,25 @@
     return {"tm": (place // 2) * LOW + lax.rem(tm, LOW), "space": lax.rem(place, 2)}
 
 
-def wide_place():
-    return ((lax.axis_index("tm") // LOW) * 2 + lax.axis_index("space")) * 2 + lax.axis_index("clip")
-
-
-def wide_peer(step):
+def plane_place():
+    return lax.axis_index("tm") // 2
+
+
+def plane_peer(step):
     tm = lax.axis_index("tm")
-    place = lax.rem(wide_place() + step, WIDE)
+    return {"tm": lax.rem(tm // 2 + step, PLANE) * 2 + lax.rem(tm, 2)}
+
+
+def column_place():
+    core = lax.rem(lax.axis_index("tm"), 2)
+    return (core * 2 + lax.axis_index("space")) * 2 + lax.axis_index("clip")
+
+
+def column_peer(step):
+    tm = lax.axis_index("tm")
+    place = lax.rem(column_place() + step, COLUMN)
     return {
-        "tm": (place // 4) * LOW + lax.rem(tm, LOW),
+        "tm": (tm // 2) * 2 + place // 4,
         "space": lax.rem(place // 2, 2),
         "clip": lax.rem(place, 2),
     }
@@ -98,36 +110,67 @@
     target[f, r * W : (r + 1) * W, L : 2 * L] = jnp.where(left, turned, below).astype(BF16)
 
 
-def conv(windows, weights, t):
+def dot_turned(a, b):
+    return lax.dot_general(a, b, (((1,), (1,)), ((), ())), preferred_element_type=F32)
+
+
+def dot(a, b):
+    return jnp.dot(a, b, preferred_element_type=F32)
+
+
+def conv(windows, weights, t, multiply):
     total = None
     for dt in range(3):
         for dr in range(3):
-            part = jnp.dot(
-                windows[t + dt, dr * W : (dr + R) * W, :],
-                weights[dt * 3 + dr],
-                preferred_element_type=F32,
-            )
+            part = multiply(windows[t + dt, dr * W : (dr + R) * W, :], weights[dt * 3 + dr])
             total = part if total is None else total + part
     return total
 
 
+def put_kernels(raw, padded, ahead, back):
+    width = 27 * C
+    padded[:, 0:width] = raw[...].astype(F32)
+    padded[:, width:] = jnp.zeros((C, padded.shape[1] - width), F32)
+    lane = lanes((C, 4 * C))
+    for tap in range(9):
+        start = tap * 3 * C
+        if tap % 2 == 0:
+            near = jnp.where(lane < 3 * C, padded[:, start : start + 4 * C], 0.0)
+            later = pltpu.roll(near, C, 1)
+        else:
+            later = jnp.where(lane < C, 0.0, padded[:, start - C : start + 3 * C])
+            near = pltpu.roll(later, 3 * C, 1)
+        near, later = near.astype(BF16), later.astype(BF16)
+        ahead[tap, 0:C, :] = near
+        ahead[tap, C : 2 * C, :] = later
+        back[8 - tap, 0:C, :] = near[:, 2 * C :]
+        back[8 - tap, C : 2 * C, :] = later[:, 2 * C :]
+        back[8 - tap, 2 * C : 3 * C, :] = near[:, 0 : 2 * C]
+        back[8 - tap, 3 * C : 4 * C, :] = later[:, 0 : 2 * C]
+
+
+def sigmoid(value):
+    return 0.5 + 0.5 * jnp.tanh(0.5 * value)
+
+
 def transposed(source):
     return source.T.astype(BF16)
 
 
 def kernel(
-    video, cot, w_first, w_second, b_first, b_second, w_down, b_down,
-    out_down, out_video, out_first, out_second, out_grad_down,
+    video, cot, raw_first, raw_second, w_down,
+    out_down, out_video, all_sd, all_f,
+    padded, w_first, w_second, b_first, b_second, b_down,
     v_ext, field, c_ext, c_field, c_win, g_block, g_ext, h_ext, t2_ext, t1, win_first, win_second,
     win_back, b_ext, b_even, b_odd, gt, gtc, st_src, st_buf,
-    full_sd, send_sd, recv_sd, sum_sd, recvb_sd, total_sd, gather_sd, all_sd,
-    full_f, send_f, recv_f, sum_f, recvb_f, total_f, gather_f, all_f,
-    halo_sems, st_sems, wa_sems, wb_sems, wc_sems, wd_sems,
+    full_sd, send_sd, recv_sd, sum_sd, recvb_sd,
+    full_f, send_f, recv_f, sum_f, recvb_f,
+    halo_sems, st_sems, wa_sems, wb_sems, wc_sems,
 ):
     tm, space = lax.axis_index("tm"), lax.axis_index("space")
     low = lax.rem(tm, LOW)
     high = (tm // LOW) * 2 + space
-    place = wide_place()
+    plane, column = plane_place(), column_place()
     has_past = jnp.where(tm == 0, 0.0, 1.0).astype(F32)
     has_next = jnp.where(tm == TM - 1, 0.0, 1.0).astype(F32)
     has_above = jnp.where(space == 0, 0.0, 1.0).astype(F32)
@@ -140,7 +183,8 @@
     edge = pl.multiple_of((R - (R - 1) * space) * W, W)
     far = pl.multiple_of((R + 1) * space * W, W)
 
-    peers = [low_peer(k) for k in range(1, LOW)] + [wide_peer(k) for k in range(1, WIDE)]
+    peers = [low_peer(k) for k in range(1, LOW)] + [high_peer(k) for k in range(1, HIGH)]
+    peers += [plane_peer(k) for k in range(1, PLANE)] + [column_peer(k) for k in range(1, COLUMN)]
     peers += [near(1, False), near(-1, False), near(1, True), near(-1, True)]
     barrier = pltpu.get_barrier_semaphore()
     for peer in peers:
@@ -231,11 +275,17 @@
         halo(4, c_ext.at[0:T, pl.ds(0, W)], c_ext.at[0:T, pl.ds(2 * W, W)], near(0, True)),
         halo(5, c_ext.at[0:2, pl.ds(0, W)], c_ext.at[T : T + 2, pl.ds(2 * W, W)], near(-1, True)),
     ])
+    put_kernels(raw_first, padded, w_first, b_first)
+    put_stats(0, 1, *join_stats(0, 0, stats, True))
+    stats = send_stats(0, 1)
     for half in range(2):
         both = c_field[2 * half : 2 * half + 2].reshape(4 * W, L)
         gtc[:, half * 4 * W : half * 4 * W + 4 * W] = transposed(both)
-    put_stats(0, 1, *join_stats(0, 0, stats, True))
-    stats = send_stats(0, 1)
+    for tap in range(9):
+        b_down[8 - tap, 0:C, 0:L] = w_down[tap, C : 2 * C, :]
+        b_down[8 - tap, 0:C, L : 2 * L] = jnp.zeros((C, L), BF16)
+        b_down[8 - tap, C : 2 * C, 0:L] = w_down[tap, 2 * C : 3 * C, :]
+        b_down[8 - tap, C : 2 * C, L : 2 * L] = w_down[tap, 0:C, :]
     ends(cot_halo)
 
     @pl.loop(0, T + 2)
@@ -254,9 +304,9 @@
         for j in range(3):
             here = c_win[t + j, 0 : 2 * W, :]
             below = c_win[t + j, W : 3 * W, :]
-            a = jnp.dot(here, b_down[j * 3 + 1], preferred_element_type=F32)
-            b = jnp.dot(here, b_down[j * 3], preferred_element_type=F32)
-            b = b + jnp.dot(below, b_down[j * 3 + 2], preferred_element_type=F32)
+            a = dot_turned(here, b_down[j * 3 + 1])
+            b = dot_turned(here, b_down[j * 3])
+            b = b + dot_turned(below, b_down[j * 3 + 2])
             even, odd = (a, b) if j == 0 else (even + a, odd + b)
         for i in range(2):
             for parity, value in ((0, even), (1, odd)):
@@ -270,10 +320,6 @@
         halo(7, g_ext.at[0:T, pl.ds(edge, W)], g_ext.at[0:T, pl.ds(far, W)], near(0, True)),
         halo(8, g_ext.at[0:2, pl.ds(edge, W)], g_ext.at[T : T + 2, pl.ds(far, W)], near(-1, True)),
     ])
-    for half in range(2):
-        both = g_ext[2 * half : 2 * half + 2, W : (R + 1) * W, :].reshape(8 * W, L)
-        gt[:, half * 8 * W : (half + 1) * 8 * W] = transposed(both.astype(F32))
-
     centre_one, scale_one = scale_of(*join_stats(0, 1, stats, True))
     ends(video_halo)
 
@@ -282,10 +328,10 @@
         early = jnp.where(f < 2, has_past, one)
         for r in range(R + 2):
             normed = (v_ext[f, r * W : (r + 1) * W, :].astype(F32) - centre_one) * scale_one
-            put_windows(win_first, f, r, normed * jax.nn.sigmoid(normed) * (early * row_mask(r)))
+            put_windows(win_first, f, r, normed * sigmoid(normed) * (early * row_mask(r)))
 
     def first_conv(t, total):
-        hidden = conv(win_first, w_first, t).astype(BF16)
+        hidden = conv(win_first, w_first, t, dot_turned).astype(BF16)
         h_ext[t + 2, W : (R + 1) * W, :] = hidden
         return total + jnp.sum(hidden.astype(F32), axis=0, keepdims=True)
 
@@ -304,6 +350,7 @@
         halo(13, h_ext.at[2:4, pl.ds(edge, W)], h_ext.at[T + 2 : T + 4, pl.ds(far, W)], near(-1, True)),
     ])
 
+    put_kernels(raw_second, padded, w_second, b_second)
     ends(grad_halo)
 
     @pl.loop(0, T + 2)
@@ -318,7 +365,7 @@
 
     @pl.loop(0, T)
     def _(t):
-        t2_ext[t, W : (R + 1) * W, :] = conv(win_back, b_second, t)
+        t2_ext[t, W : (R + 1) * W, :] = conv(win_back, b_second, t, dot)
 
     act_halo = begins([
         halo(14, t2_ext.at[0:2, own], t2_ext.at[T : T + 2, own], near(-1, False)),
@@ -326,10 +373,14 @@
         halo(16, t2_ext.at[0:2, pl.ds(edge, W)], t2_ext.at[T : T + 2, pl.ds(far, W)], near(-1, True)),
     ])
 
+    for half in range(2):
+        both = g_ext[2 * half : 2 * half + 2, W : (R + 1) * W, :].reshape(8 * W, L)
+        gt[:, half * 8 * W : (half + 1) * 8 * W] = transposed(both.astype(F32))
+
     centre_two, scale_two = scale_of(*join_stats(1, 1, stats, True))
 
     def gradient(grad, normed):
-        sigma = jax.nn.sigmoid(normed)
+        sigma = sigmoid(normed)
         return grad * sigma * (1.0 + normed * (1.0 - sigma))
 
     def second_sums(t, sums):
@@ -351,14 +402,14 @@
         early = jnp.where(f < 2, has_past, one)
         for r in range(R + 2):
             normed = (h_ext[f, r * W : (r + 1) * W, :].astype(F32) - centre_two) * scale_two
-            put_windows(win_second, f, r, normed * jax.nn.sigmoid(normed) * (early * row_mask(r)))
+            put_windows(win_second, f, r, normed * sigmoid(normed) * (early * row_mask(r)))
 
     put_stats(2, 1, *join_stats(2, 0, stats, False))
     stats = send_stats(2, 1)
 
     @pl.loop(0, T)
     def _(t):
-        block = v_ext[t + 2, W : (R + 1) * W, :].astype(F32) + conv(win_second, w_second, t)
+        block = v_ext[t + 2, W : (R + 1) * W, :].astype(F32) + conv(win_second, w_second, t, dot_turned)
         b_ext[t + 2, W : (R + 1) * W, :] = block.astype(BF16)
 
     block_halo = begins([
@@ -367,26 +418,30 @@
         halo(19, b_ext.at[T : T + 2, pl.ds(R * W, W)], b_ext.at[0:2, pl.ds(0, W)], near(1, True)),
     ])
 
-    def block_weights(windows, full, base):
-        left = lanes((3 * C, L)) < C
-
-        def folded(dt, dr):
+    def block_weights(windows, full):
+        left = lanes((C, L)) < C
+
+        def folded(tap):
+            dt, dr = tap // 3, tap % 3
             cells = windows[dt : dt + T, dr * W : (dr + R) * W, :].reshape(CELLS, 2 * L)
-            turned = jnp.dot(gt[...], cells, preferred_element_type=F32).T
-            return turned[0 : 3 * C] + pltpu.roll(turned[C : 4 * C], C, 1)
+            both = dot(gt[...], cells)
+            return both[0:C] + pltpu.roll(both[C : 2 * C], 3 * C, 1)
+
+        def put(tile, value):
+            full[tile * C : (tile + 1) * C, :] = value
 
         for pair in range(4):
-            a, b = 2 * pair, 2 * pair + 1
-            value = jnp.where(left, folded(a // 3, a % 3), pltpu.roll(folded(b // 3, b % 3), C, 1))
-            full[base + pair * 3 * C : base + (pair + 1) * 3 * C, :] = value
-        value = folded(2, 2)
-        half = 3 * C // 2
-        value = jnp.where(left[0:half], value[0:half], pltpu.roll(value[half:], C, 1))
-        full[base + 12 * C : base + 12 * C + half, :] = value
+            a, b = folded(2 * pair), pltpu.roll(folded(2 * pair + 1), C, 1)
+            put(3 * pair, a[:, 0:L])
+            put(3 * pair + 1, jnp.where(left, a[:, L : 2 * L], b[:, 0:L]))
+            put(3 * pair + 2, b[:, L : 2 * L])
+        value = folded(8)
+        put(12, value[:, 0:L])
+        put(13, jnp.where(left, value[:, L : 2 * L], 0.0))
 
     full_sd[HALF + 27 * C :, :] = jnp.zeros((full_sd.shape[0] - HALF - 27 * C, L), F32)
     full_f[HALF:, :] = jnp.zeros((full_f.shape[0] - HALF, L), F32)
-    block_weights(win_second, full_sd, 0)
+    block_weights(win_second, full_sd)
 
     ends(block_halo)
 
@@ -399,22 +454,6 @@
 
     def projected(dr):
         return (b_even, 0) if dr == 0 else (b_odd, 0) if dr == 1 else (b_even, W)
-
-    @pl.loop(0, T)
-    def _(t):
-        total = None
-        for dt in range(3):
-            for dr in range(3):
-                ref, start = projected(dr)
-                part = jnp.dot(
-                    ref[t + dt, start : start + 2 * W, 0 : 3 * C],
-                    w_down[dt * 3 + dr],
-                    preferred_element_type=F32,
-                )
-                total = part if total is None else total + part
-        c_field[t] = total
-        for p in range(W):
-            out_down[0, t, :, p * L : (p + 1) * L] = c_field[t, pl.ds(p, 2, stride=W), :].astype(BF16)
 
     for dt in range(3):
         for dr in range(3):
@@ -424,74 +463,58 @@
             base = HALF + (dt * 3 + dr) * 3 * C
             full_sd[base : base + 3 * C, :] = turned[0 : 3 * C]
 
-    def part_of(index, rows):
-        return pl.ds(pl.multiple_of(index * rows, 8), rows)
-
     class Reduction:
-        def __init__(self, number, piece, full, send, recv, sums, recvb, total, gather, whole):
-            self.n, self.piece, self.rows = number, piece, piece * WIDE
+        def __init__(self, number, piece, full, send, recv, sums, recvb, whole):
+            self.n, self.piece = number, piece
             self.full, self.send, self.recv, self.sums = full, send, recv, sums
-            self.recvb, self.total, self.gather, self.whole = recvb, total, gather, whole
+            self.recvb, self.whole = recvb, whole
 
         def sem(self, sems, k):
             return sems.at[0, self.n, k], sems.at[1, self.n, k]
+
+        def part(self, index):
+            return pl.ds(pl.multiple_of(index * self.piece, 16), self.piece)
 
         def start(self):
             self.send[...] = self.full[...].astype(BF16)
             self.copies = begins([
                 remote(
-                    self.send.at[part_of(lax.rem(low + k, LOW), self.rows)], self.recv.at[k - 1],
-                    *self.sem(wa_sems, k), low_peer(k),
+                    self.send.at[self.part(lax.rem(plane + k, PLANE))], self.recv.at[k - 1],
+                    *self.sem(wa_sems, k), plane_peer(k),
                 )
-                for k in range(1, LOW)
+                for k in range(1, PLANE)
             ])
 
         def second(self):
             ends(self.copies)
-            value = self.full[part_of(low, self.rows), :]
-            for k in range(LOW - 1):
+            value = self.full[self.part(plane), :]
+            for k in range(PLANE - 1):
                 value = value + self.recv[k].astype(F32)
             self.sums[...] = value
             self.copies = begins([
-                remote(
-                    self.sums.at[part_of(lax.rem(place + k, WIDE), self.piece)], self.recvb.at[k - 1],
-                    *self.sem(wb_sems, k), wide_peer(k),
-                )
-                for k in range(1, WIDE)
+                remote(self.sums, self.recvb.at[column], *self.sem(wb_sems, k), column_peer(k))
+                for k in range(1, COLUMN)
             ])
+            self.recvb[column] = value
 
         def third(self):
             ends(self.copies)
-            value = self.sums[part_of(place, self.piece), :]
-            for k in range(WIDE - 1):
+            value = self.recvb[0]
+            for k in range(1, COLUMN):
                 value = value + self.recvb[k]
             value = value * (1.0 / math.sqrt(2 * 128 * 8 * 160))
-            self.total[...] = value
+            here = self.part(plane)
+            self.whole[here, :] = value.astype(BF16)
             self.copies = begins([
-                remote(
-                    self.total, self.gather.at[part_of(place, self.piece)],
-                    *self.sem(wc_sems, k), wide_peer(k),
-                )
-                for k in range(1, WIDE)
-            ])
-            self.gather[part_of(place, self.piece), :] = value
-
-        def fourth(self):
-            ends(self.copies)
-            here = pl.ds(pl.multiple_of(low * self.rows, 16), self.rows)
-            self.whole[here, :] = self.gather[...].astype(BF16)
-            self.copies = begins([
-                remote(
-                    self.whole.at[here], self.whole.at[here], *self.sem(wd_sems, k), low_peer(k),
-                )
-                for k in range(1, LOW)
+                remote(self.whole.at[here], self.whole.at[here], *self.sem(wc_sems, k), plane_peer(k))
+                for k in range(1, PLANE)
             ])
 
         def finish(self):
             ends(self.copies)
 
-    sums_sd = Reduction(0, PIECE_SD, full_sd, send_sd, recv_sd, sum_sd, recvb_sd, total_sd, gather_sd, all_sd)
-    sums_f = Reduction(1, PIECE_F, full_f, send_f, recv_f, sum_f, recvb_f, total_f, gather_f, all_f)
+    sums_sd = Reduction(0, PIECE_SD, full_sd, send_sd, recv_sd, sum_sd, recvb_sd, all_sd)
+    sums_f = Reduction(1, PIECE_F, full_f, send_f, recv_f, sum_f, recvb_f, all_f)
     sums_sd.start()
 
     count = 1.0 / (4 * GROUP_CELLS)
@@ -513,8 +536,15 @@
                 def _():
                     field[f, (r - 1) * W : r * W, :] = hidden
 
+    for half in range(2):
+        both = field[2 * half : 2 * half + 2].reshape(8 * W, L)
+        gt[:, half * 8 * W : (half + 1) * 8 * W] = transposed(both)
+    block_weights(win_first, full_f)
+    sums_f.start()
+    sums_sd.second()
+
     def back_first(t, sums):
-        back = conv(win_back, b_first, t)
+        back = conv(win_back, b_first, t, dot)
         normed = (v_ext[t + 2, W : (R + 1) * W, :].astype(F32) - centre_one) * scale_one
         grad = gradient(back, normed)
         t1[t] = grad
@@ -525,102 +555,84 @@
 
     put_stats(3, 0, *lax.fori_loop(0, T, back_first, nothing))
     stats = send_stats(3, 0)
-    sums_sd.second()
-    for half in range(2):
-        both = field[2 * half : 2 * half + 2].reshape(8 * W, L)
-        gt[:, half * 8 * W : (half + 1) * 8 * W] = transposed(both)
-    block_weights(win_first, full_f, 0)
-    sums_f.start()
+    sums_f.second()
+
+    @pl.loop(0, T)
+    def _(t):
+        total = None
+        for dt in range(3):
+            for dr in range(3):
+                ref, start = projected(dr)
+                part = dot(ref[t + dt, start : start + 2 * W, 0 : 3 * C], w_down[dt * 3 + dr])
+                total = part if total is None else total + part
+        out_down[t] = total
+
     put_stats(3, 1, *join_stats(3, 0, stats, False))
     stats = send_stats(3, 1)
     sums_sd.third()
-    sums_f.second()
+    sums_f.third()
     first, second = join_stats(3, 1, stats, False)
     mean_one, mean_two = over_group(first) * count, over_group(second) * count
-    sums_sd.fourth()
 
     @pl.loop(0, T)
     def _(t):
         normed = (v_ext[t + 2, W : (R + 1) * W, :].astype(F32) - centre_one) * scale_one
-        field[t] = g_block[t] + scale_one * (t1[t] - mean_one - normed * mean_two)
-        for p in range(W):
-            out_video[0, t, :, p * L : (p + 1) * L] = field[t, pl.ds(p, R, stride=W), :]
-
-    sums_f.third()
-    sums_f.fourth()
-
-    def unpack(source, base, target):
-        for pair in range(4):
-            value = source[base + pair * 3 * C : base + (pair + 1) * 3 * C, :].astype(F32)
-            target[pair * 6 * C : pair * 6 * C + 3 * C, :] = value[:, 0:C]
-            target[pair * 6 * C + 3 * C : (pair + 1) * 6 * C, :] = pltpu.roll(value, C, 1)[:, 0:C]
-        half = 3 * C // 2
-        value = source[base + 12 * C : base + 12 * C + half, :].astype(F32)
-        target[24 * C : 24 * C + half, :] = value[:, 0:C]
-        target[24 * C + half : 27 * C, :] = pltpu.roll(value, C, 1)[:, 0:C]
+        out_video[t] = g_block[t] + scale_one * (t1[t] - mean_one - normed * mean_two)
 
     sums_sd.finish()
-    unpack(all_sd, 0, out_second)
-    out_grad_down[...] = all_sd[HALF : HALF + 27 * C, :].astype(F32)
     sums_f.finish()
-    unpack(all_f, 0, out_first)
-
-
-def windowed(kernels):
-    flat = kernels.reshape(9, 3 * C, C)
-    empty = jnp.zeros((9, C, C), flat.dtype)
-    return jnp.concatenate(
-        [jnp.concatenate([flat, empty], axis=1), jnp.concatenate([empty, flat], axis=1)], axis=2
-    )
-
-
-def flipped(weight, channels):
-    return jnp.swapaxes(weight.reshape(27, C, channels)[::-1], 1, 2)
+
+
+def finish_kernel(down, video, sums_sd, sums_f, out_down, out_video, out_first, out_second, out_grad_down):
+    for p in range(W):
+        here = slice(p * L, (p + 1) * L)
+        out_video[0, 0, :, here] = video[0, pl.ds(p, R, stride=W), :]
+        out_down[0, 0, :, here] = down[0, pl.ds(p, 2, stride=W), :].astype(BF16)
+
+    @pl.when(pl.program_id(0) == 0)
+    def _():
+        for source, target in ((sums_sd, out_second), (sums_f, out_first)):
+            for tile in range(TILES):
+                width = min(L, 27 * C - tile * L)
+                value = source[tile * C : (tile + 1) * C, :].astype(F32)
+                target[:, tile * L : tile * L + width] = value[:, 0:width]
+        out_grad_down[...] = sums_sd[HALF : HALF + 27 * C, :].astype(F32)
 
 
 def local(video, conv_first, conv_second, conv_down, down_cotangent):
-    back_down = flipped(conv_down, C_OUT).reshape(9, 3, C_OUT, C)
-    upper = jnp.concatenate([back_down[:, 1], back_down[:, 0]], axis=2)
-    lower = jnp.concatenate([jnp.zeros_like(back_down[:, 2]), back_down[:, 2]], axis=2)
     operands = (
-        video,
-        down_cotangent,
-        windowed(conv_first.reshape(9, 3, C, C)),
-        windowed(conv_second.reshape(9, 3, C, C)),
-        windowed(flipped(conv_first, C).reshape(9, 3, C, C)),
-        windowed(flipped(conv_second, C).reshape(9, 3, C, C)),
-        conv_down.reshape(9, 3 * C, C_OUT),
-        jnp.concatenate([upper, lower], axis=1),
+        video, down_cotangent, conv_first.T, conv_second.T, conv_down.reshape(9, 3 * C, C_OUT)
     )
     rows = (R + 2) * W
 
     def reduction(piece):
-        total, part = piece * WIDE * LOW, piece * WIDE
         return [
-            pltpu.VMEM((total, L), F32),
-            pltpu.VMEM((total, L), BF16),
-            pltpu.VMEM((LOW - 1, part, L), BF16),
-            pltpu.VMEM((part, L), F32),
-            pltpu.VMEM((WIDE - 1, piece, L), F32),
+            pltpu.VMEM((piece * PLANE, L), F32),
+            pltpu.VMEM((piece * PLANE, L), BF16),
+            pltpu.VMEM((PLANE - 1, piece, L), BF16),
             pltpu.VMEM((piece, L), F32),
-            pltpu.VMEM((part, L), F32),
-            pltpu.VMEM((total, L), BF16),
+            pltpu.VMEM((COLUMN, piece, L), F32),
         ]
 
     vmem = pl.BlockSpec(memory_space=pltpu.VMEM)
     dma = pltpu.SemaphoreType.DMA
-    return pl.pallas_call(
+    results = pl.pallas_call(
         kernel,
         out_shape=(
-            jax.ShapeDtypeStruct((1, T, 2, W * L), BF16),
-            jax.ShapeDtypeStruct((1, T, R, W * L), F32),
-            jax.ShapeDtypeStruct((27 * C, C), F32),
-            jax.ShapeDtypeStruct((27 * C, C), F32),
-            jax.ShapeDtypeStruct((27 * C, C_OUT), F32),
+            jax.ShapeDtypeStruct((T, 2 * W, L), F32),
+            jax.ShapeDtypeStruct((T, R * W, L), F32),
+            jax.ShapeDtypeStruct((PIECE_SD * PLANE, L), BF16),
+            jax.ShapeDtypeStruct((PIECE_F * PLANE, L), BF16),
         ),
         in_specs=[vmem] * len(operands),
-        out_specs=(vmem,) * 5,
+        out_specs=(vmem,) * 4,
         scratch_shapes=[
+            pltpu.VMEM((C, TILES * L), F32),
+            pltpu.VMEM((9, 2 * C, 4 * C), BF16),
+            pltpu.VMEM((9, 2 * C, 4 * C), BF16),
+            pltpu.VMEM((9, 4 * C, 2 * C), BF16),
+            pltpu.VMEM((9, 4 * C, 2 * C), BF16),
+            pltpu.VMEM((9, 2 * C, 2 * C_OUT), BF16),
             pltpu.VMEM((T + 2, rows, L), BF16),
             pltpu.VMEM((T, R * W, L), F32),
             pltpu.VMEM((T + 2, 3 * W, L), BF16),
@@ -645,16 +657,47 @@
             *reduction(PIECE_F),
             dma((2, 20)),
             dma((2, 4, 2, LOW)),
-            dma((2, 2, LOW)),
-            dma((2, 2, WIDE)),
-            dma((2, 2, WIDE)),
-            dma((2, 2, LOW)),
+            dma((2, 2, PLANE)),
+            dma((2, 2, COLUMN)),
+            dma((2, 2, PLANE)),
         ],
         compiler_params=pltpu.CompilerParams(
             collective_id=1, has_side_effects=True, vmem_limit_bytes=56 * 1024 * 1024
         ),
     )(*operands)
 
+    def frame(*shape):
+        return pl.BlockSpec(shape, lambda t: (t,) + (0,) * (len(shape) - 1))
+
+    def out_frame(rows):
+        return pl.BlockSpec((1, 1, rows, W * L), lambda t: (0, t, 0, 0))
+
+    def whole(*shape):
+        return pl.BlockSpec(shape, lambda t: (0,) * len(shape))
+
+    down, grad_video, first, second, grad_down = pl.pallas_call(
+        finish_kernel,
+        grid=(T,),
+        out_shape=(
+            jax.ShapeDtypeStruct((1, T, 2, W * L), BF16),
+            jax.ShapeDtypeStruct((1, T, R, W * L), F32),
+            jax.ShapeDtypeStruct((C, 27 * C), F32),
+            jax.ShapeDtypeStruct((C, 27 * C), F32),
+            jax.ShapeDtypeStruct((27 * C, C_OUT), F32),
+        ),
+        in_specs=[
+            frame(1, 2 * W, L),
+            frame(1, R * W, L),
+            whole(PIECE_SD * PLANE, L),
+            whole(PIECE_F * PLANE, L),
+        ],
+        out_specs=(
+            out_frame(2), out_frame(R), whole(C, 27 * C), whole(C, 27 * C), whole(27 * C, C_OUT)
+        ),
+        compiler_params=pltpu.CompilerParams(vmem_limit_bytes=32 * 1024 * 1024),
+    )(*results)
+    return down, grad_video, first.T, second.T, grad_down
+
 
 def solution(mesh):
     in_specs = (P("clip", "tm", "space", None), P(), P(), P(), P("clip", "tm", "space", None))

time: 105 us -> 94.4 us (0.90)
  the two profiles are of different devices: /device:TPU:1 before, /device:TPU:65 now
where the time goes in v2:
time: 94.4 us; the launch traced here: 94.2 us
  Pallas kernels  89.4 us (95%)
  local copies, waits for them, and re-layouts  4.11 us (4%)
    pallas_call x1, Pallas kernels, local(): pl.pallas_call(kernel, out_shape=(jax.ShapeDtypeStruct((T, 2 * W, L), F32...  87 us
    unnamed x8, local copies, waits for them, and re-layouts  4.11 us
    pallas_call x1, Pallas kernels, local(): pl.pallas_call(finish_kernel, grid=(T,), out_shape=(jax.ShapeDtypeStruct(...  2.43 us

profile of v2, /device:TPU:65, one launch (start us, length us, event | category | flops | bytes accessed | tf_op | source)
XLA Modules:
  0.0 94.2 jit_solution(15858789001925877541)
XLA Ops:
  0.6 87.0 %shard_map.92 = (f32[4,160,128]{2,1,0:T(8,128)}, f32[4,320,128]{2,1,0:T(8,128)}, bf16[2816,128]{1,0:T(8,128)(2,1)}, bf16[1024,128]{1,0:T(8,128)(2,1)}) custom-call(bf16[1,4,4,10240]{3,2,1,0:T(4,128)(2,1)} %video.1, bf16[1,4,2,10240]{3,2,1,0:T(2,128)(2,1)} %cot.1, bf16[64,1728]{1,0:T(8,128)(2,1)} %bitcast.6, bf16[64,1728]{1,0:T(8,128)(2,1)} %bitcast.7, ...), custom_call_target="tpu_custom_call" | custom-call | tf_op jit(solution)/shard_map/pallas_call | solution.py:619
  87.6 0.0 copy-start
  87.6 1.1 %copy-done = bf16[2816,128]{1,0:T(8,128)(2,1)S(1)} copy-done((bf16[2816,128]{1,0:T(8,128)(2,1)S(1)}, bf16[2816,128]{1,0:T(8,128)(2,1)}, u32[]{:S(2)}) %copy-start) | copy-done | bytes 720920
  88.7 0.0 copy-start.1
  88.7 1.1 %copy-done.1 = f32[4,320,128]{2,1,0:T(8,128)S(1)} copy-done((f32[4,320,128]{2,1,0:T(8,128)S(1)}, f32[4,320,128]{2,1,0:T(8,128)}, u32[]{:S(2)}) %copy-start.1) | copy-done | bytes 655384
  89.8 0.0 copy-start.2
  89.8 1.0 %copy-done.2 = f32[4,160,128]{2,1,0:T(8,128)S(1)} copy-done((f32[4,160,128]{2,1,0:T(8,128)S(1)}, f32[4,160,128]{2,1,0:T(8,128)}, u32[]{:S(2)}) %copy-start.2) | copy-done | bytes 327704
  90.8 0.0 copy-start.3
  90.8 0.9 %copy-done.3 = bf16[1024,128]{1,0:T(8,128)(2,1)S(1)} copy-done((bf16[1024,128]{1,0:T(8,128)(2,1)S(1)}, bf16[1024,128]{1,0:T(8,128)(2,1)}, u32[]{:S(2)}) %copy-start.3) | copy-done | bytes 262168
  91.7 2.4 %shard_map.93 = (bf16[1,4,2,10240]{3,2,1,0:T(2,128)(2,1)}, f32[1,4,4,10240]{3,2,1,0:T(4,128)}, f32[64,1728]{1,0:T(8,128)}, f32[64,1728]{1,0:T(8,128)}, f32[1728,128]{1,0:T(8,128)}) custom-call(f32[4,160,128]{2,1,0:T(8,128)S(1)} %copy-done.2, f32[4,320,128]{2,1,0:T(8,128)S(1)} %copy-done.1, bf16[2816,128]{1,0:T(8,128)(2,1)S(1)} %copy-done, ...), custom_call_target="tpu_custom_call" | custom-call | tf_op jit(solution)/shard_map/pallas_call | solution.py:678
Async XLA Ops:
  87.6 1.1 %copy-start = (bf16[2816,128]{1,0:T(8,128)(2,1)S(1)}, bf16[2816,128]{1,0:T(8,128)(2,1)}, u32[]{:S(2)}) copy-start(bf16[2816,128]{1,0:T(8,128)(2,1)} %get-tuple-element.16.sums_sd) | copy-start | bytes 2162692
  88.7 1.1 %copy-start.1 = (f32[4,320,128]{2,1,0:T(8,128)S(1)}, f32[4,320,128]{2,1,0:T(8,128)}, u32[]{:S(2)}) copy-start(f32[4,320,128]{2,1,0:T(8,128)} %get-tuple-element.15.video) | copy-start | bytes 1966084
  89.8 1.0 %copy-start.2 = (f32[4,160,128]{2,1,0:T(8,128)S(1)}, f32[4,160,128]{2,1,0:T(8,128)}, u32[]{:S(2)}) copy-start(f32[4,160,128]{2,1,0:T(8,128)} %get-tuple-element.14.down) | copy-start | bytes 983044
  90.8 0.9 %copy-start.3 = (bf16[1024,128]{1,0:T(8,128)(2,1)S(1)}, bf16[1024,128]{1,0:T(8,128)(2,1)}, u32[]{:S(2)}) copy-start(bf16[1024,128]{1,0:T(8,128)(2,1)} %get-tuple-element.17.sums_f) | copy-start | bytes 786436

commit v3 on v2

--- a/solution.py
+++ b/solution.py
@@ -118,13 +118,18 @@
     return jnp.dot(a, b, preferred_element_type=F32)
 
 
-def conv(windows, weights, t, multiply):
-    total = None
-    for dt in range(3):
+def conv(windows, weights, total, multiply):
+    total[...] = jnp.zeros_like(total)
+
+    @pl.loop(0, 4)
+    def _(o):
+        value = None
         for dr in range(3):
-            part = multiply(windows[t + dt, dr * W : (dr + R) * W, :], weights[dt * 3 + dr])
-            total = part if total is None else total + part
-    return total
+            rows = slice(dr * W, (dr + R) * W)
+            both = jnp.concatenate([windows[o, rows, :], windows[o + 2, rows, :]], axis=0)
+            part = multiply(both, weights[o, dr])
+            value = part if value is None else value + part
+        total[...] = total[...] + value
 
 
 def put_kernels(raw, padded, ahead, back):
@@ -132,6 +137,11 @@
     padded[:, 0:width] = raw[...].astype(F32)
     padded[:, width:] = jnp.zeros((C, padded.shape[1] - width), F32)
     lane = lanes((C, 4 * C))
+    for dr in range(3):
+        ahead[0, dr, 2 * C : 4 * C, :] = jnp.zeros((2 * C, 4 * C), BF16)
+        ahead[3, dr, 0 : 2 * C, :] = jnp.zeros((2 * C, 4 * C), BF16)
+        back[0, dr, :, 2 * C : 4 * C] = jnp.zeros((4 * C, 2 * C), BF16)
+        back[3, dr, :, 0 : 2 * C] = jnp.zeros((4 * C, 2 * C), BF16)
     for tap in range(9):
         start = tap * 3 * C
         if tap % 2 == 0:
@@ -141,12 +151,17 @@
             later = jnp.where(lane < C, 0.0, padded[:, start - C : start + 3 * C])
             near = pltpu.roll(later, 3 * C, 1)
         near, later = near.astype(BF16), later.astype(BF16)
-        ahead[tap, 0:C, :] = near
-        ahead[tap, C : 2 * C, :] = later
-        back[8 - tap, 0:C, :] = near[:, 2 * C :]
-        back[8 - tap, C : 2 * C, :] = later[:, 2 * C :]
-        back[8 - tap, 2 * C : 3 * C, :] = near[:, 0 : 2 * C]
-        back[8 - tap, 3 * C : 4 * C, :] = later[:, 0 : 2 * C]
+        dt, dr = tap // 3, tap % 3
+        for frame in range(2):
+            base = frame * 2 * C
+            ahead[dt + frame, dr, base : base + C, :] = near
+            ahead[dt + frame, dr, base + C : base + 2 * C, :] = later
+            target = back.at[2 - dt + frame, 2 - dr]
+            here = slice(base, base + 2 * C)
+            target[0:C, here] = near[:, 2 * C :]
+            target[C : 2 * C, here] = later[:, 2 * C :]
+            target[2 * C : 3 * C, here] = near[:, 0 : 2 * C]
+            target[3 * C : 4 * C, here] = later[:, 0 : 2 * C]
 
 
 def sigmoid(value):
@@ -160,8 +175,8 @@
 def kernel(
     video, cot, raw_first, raw_second, w_down,
     out_down, out_video, all_sd, all_f,
-    padded, w_first, w_second, b_first, b_second, b_down,
-    v_ext, field, c_ext, c_field, c_win, g_block, g_ext, h_ext, t2_ext, t1, win_first, win_second,
+    padded, w_first, w_second, b_first, b_second, b_down, wide,
+    v_ext, field, c_ext, c_field, c_win, g_block, h_ext, t2_ext, t2, t1, win_first, win_second,
     win_back, b_ext, b_even, b_odd, gt, gtc, st_src, st_buf,
     full_sd, send_sd, recv_sd, sum_sd, recvb_sd,
     full_f, send_f, recv_f, sum_f, recvb_f,
@@ -200,7 +215,7 @@
         return remote(source, target, halo_sems.at[0, slot], halo_sems.at[1, slot], device)
 
     def send_stats(k, stage):
-        me, peer, size = (low, low_peer, LOW) if stage == 0 else (high, high_peer, HIGH)
+        me, peer, size = (high, high_peer, HIGH) if stage == 0 else (low, low_peer, LOW)
         copies = begins([
             remote(
                 st_src.at[k, stage], st_buf.at[k, stage, me],
@@ -260,7 +275,7 @@
         halo(1, v_ext.at[2 : T + 2, pl.ds(edge, W)], v_ext.at[2 : T + 2, pl.ds(far, W)], near(0, True)),
         halo(2, v_ext.at[T : T + 2, pl.ds(edge, W)], v_ext.at[0:2, pl.ds(far, W)], near(1, True)),
     ])
-    for ref in (v_ext, g_ext, h_ext, t2_ext):
+    for ref in (v_ext, h_ext, t2_ext):
         for f in range(ref.shape[0]):
             ref[f, pl.ds(far, W), :] = jnp.zeros((W, L), ref.dtype)
 
@@ -268,13 +283,18 @@
     def _(t):
         for p in range(W):
             c_field[t, pl.ds(p, 2, stride=W), :] = cot[0, t, :, p * L : (p + 1) * L].astype(F32)
-        c_ext[t, 0 : 2 * W, :] = c_field[t].astype(BF16)
-
+        c_ext[t, W : 3 * W, :] = c_field[t].astype(BF16)
+
+    c_own = pl.ds(W, 2 * W)
+    c_edge = pl.ds(pl.multiple_of((2 - space) * W, W), W)
+    c_far = pl.ds(pl.multiple_of(3 * space * W, W), W)
     cot_halo = begins([
-        halo(3, c_ext.at[0:2, pl.ds(0, 2 * W)], c_ext.at[T : T + 2, pl.ds(0, 2 * W)], near(-1, False)),
-        halo(4, c_ext.at[0:T, pl.ds(0, W)], c_ext.at[0:T, pl.ds(2 * W, W)], near(0, True)),
-        halo(5, c_ext.at[0:2, pl.ds(0, W)], c_ext.at[T : T + 2, pl.ds(2 * W, W)], near(-1, True)),
+        halo(3, c_ext.at[0:T, c_own], c_ext.at[T : 2 * T, c_own], near(-1, False)),
+        halo(4, c_ext.at[0:T, c_edge], c_ext.at[0:T, c_far], near(0, True)),
+        halo(5, c_ext.at[0:T, c_edge], c_ext.at[T : 2 * T, c_far], near(-1, True)),
     ])
+    for f in range(2 * T):
+        c_ext[f, c_far, :] = jnp.zeros((W, L), BF16)
     put_kernels(raw_first, padded, w_first, b_first)
     put_stats(0, 1, *join_stats(0, 0, stats, True))
     stats = send_stats(0, 1)
@@ -288,38 +308,38 @@
         b_down[8 - tap, C : 2 * C, L : 2 * L] = w_down[tap, 0:C, :]
     ends(cot_halo)
 
+    @pl.loop(0, 2 * T)
+    def _(f):
+        late = jnp.where(f >= T, has_next, one)
+        row = lax.broadcasted_iota(jnp.int32, (W, L), 0)
+        for r in range(4):
+            value = c_ext[f, r * W : (r + 1) * W, :].astype(F32)
+            value = value * (late * has_above if r == 0 else late * has_below if r == 3 else late)
+            after = jnp.where(row == W - 1, 0.0, pltpu.roll(value, W - 1, 0))
+            c_win[f, r * W : (r + 1) * W, 0:L] = value.astype(BF16)
+            c_win[f, r * W : (r + 1) * W, L : 2 * L] = after.astype(BF16)
+
     @pl.loop(0, T + 2)
     def _(f):
         late = jnp.where(f >= T, has_next, one)
-        for r in range(3):
-            value = c_ext[f, r * W : (r + 1) * W, :].astype(F32) * (late * has_below if r == 2 else late)
-            row = lax.broadcasted_iota(jnp.int32, (W, L), 0)
-            after = jnp.where(row == W - 1, 0.0, pltpu.roll(value, W - 1, 0))
-            c_win[f, r * W : (r + 1) * W, 0:L] = value.astype(BF16)
-            c_win[f, r * W : (r + 1) * W, L : 2 * L] = after.astype(BF16)
-
-    @pl.loop(0, T)
-    def _(t):
         even = odd = None
         for j in range(3):
-            here = c_win[t + j, 0 : 2 * W, :]
-            below = c_win[t + j, W : 3 * W, :]
-            a = dot_turned(here, b_down[j * 3 + 1])
-            b = dot_turned(here, b_down[j * 3])
-            b = b + dot_turned(below, b_down[j * 3 + 2])
+            upper = c_win[f + j, 0 : 3 * W, :]
+            lower = c_win[f + j, W : 4 * W, :]
+            a = dot_turned(lower, b_down[j * 3 + 1])
+            b = dot_turned(upper, b_down[j * 3])
+            b = b + dot_turned(lower, b_down[j * 3 + 2])
             even, odd = (a, b) if j == 0 else (even + a, odd + b)
-        for i in range(2):
-            for parity, value in ((0, even), (1, odd)):
-                r = 2 * i + parity
-                piece = value[i * W : (i + 1) * W]
-                g_block[t, r * W : (r + 1) * W, :] = piece
-                g_ext[t, (r + 1) * W : (r + 2) * W, :] = piece.astype(BF16)
-
-    grad_halo = begins([
-        halo(6, g_ext.at[0:2, own], g_ext.at[T : T + 2, own], near(-1, False)),
-        halo(7, g_ext.at[0:T, pl.ds(edge, W)], g_ext.at[0:T, pl.ds(far, W)], near(0, True)),
-        halo(8, g_ext.at[0:2, pl.ds(edge, W)], g_ext.at[T : T + 2, pl.ds(far, W)], near(-1, True)),
-    ])
+        for i in range(3):
+            for r, value in ((2 * i, odd), (2 * i + 1, even)):
+                put_windows(win_back, f, r, value[i * W : (i + 1) * W] * (late * row_mask(r)))
+
+        @pl.when(f < T)
+        def _():
+            for r in range(1, R + 1):
+                value = (even if r % 2 else odd)[(r // 2) * W : (r // 2 + 1) * W]
+                g_block[f, (r - 1) * W : r * W, :] = value
+
     centre_one, scale_one = scale_of(*join_stats(0, 1, stats, True))
     ends(video_halo)
 
@@ -330,12 +350,23 @@
             normed = (v_ext[f, r * W : (r + 1) * W, :].astype(F32) - centre_one) * scale_one
             put_windows(win_first, f, r, normed * sigmoid(normed) * (early * row_mask(r)))
 
-    def first_conv(t, total):
-        hidden = conv(win_first, w_first, t, dot_turned).astype(BF16)
+    def result(q, frame):
+        here = slice(frame * L, (frame + 1) * L)
+        return wide[q * R * W : (q + 1) * R * W, here]
+
+    def frames_of(step, start):
+        for q in range(T // 2):
+            for frame in range(2):
+                start = step(2 * q + frame, result(q, frame), start)
+        return start
+
+    def first_conv(t, value, total):
+        hidden = value.astype(BF16)
         h_ext[t + 2, W : (R + 1) * W, :] = hidden
         return total + jnp.sum(hidden.astype(F32), axis=0, keepdims=True)
 
-    mean = lax.fori_loop(0, T, first_conv, jnp.zeros((1, L), F32)) * (1.0 / CELLS)
+    conv(win_first, w_first, wide, dot_turned)
+    mean = frames_of(first_conv, jnp.zeros((1, L), F32)) * (1.0 / CELLS)
 
     def own_hidden(t):
         return h_ext[t + 2, W : (R + 1) * W, :].astype(F32)
@@ -351,21 +382,19 @@
     ])
 
     put_kernels(raw_second, padded, w_second, b_second)
-    ends(grad_halo)
-
-    @pl.loop(0, T + 2)
-    def _(f):
-        late = jnp.where(f >= T, has_next, one)
-        for r in range(R + 2):
-            value = g_ext[f, r * W : (r + 1) * W, :].astype(F32) * (late * row_mask(r))
-            put_windows(win_back, f, r, value)
+    for half in range(2):
+        both = g_block[2 * half : 2 * half + 2].reshape(8 * W, L)
+        gt[:, half * 8 * W : (half + 1) * 8 * W] = transposed(both)
 
     put_stats(1, 1, *join_stats(1, 0, stats, True))
     stats = send_stats(1, 1)
 
-    @pl.loop(0, T)
-    def _(t):
-        t2_ext[t, W : (R + 1) * W, :] = conv(win_back, b_second, t, dot)
+    def keep_back(t, value, _):
+        t2[t] = value
+        t2_ext[t, W : (R + 1) * W, :] = value.astype(BF16)
+
+    conv(win_back, b_second, wide, dot)
+    frames_of(keep_back, None)
 
     act_halo = begins([
         halo(14, t2_ext.at[0:2, own], t2_ext.at[T : T + 2, own], near(-1, False)),
@@ -373,10 +402,6 @@
         halo(16, t2_ext.at[0:2, pl.ds(edge, W)], t2_ext.at[T : T + 2, pl.ds(far, W)], near(-1, True)),
     ])
 
-    for half in range(2):
-        both = g_ext[2 * half : 2 * half + 2, W : (R + 1) * W, :].reshape(8 * W, L)
-        gt[:, half * 8 * W : (half + 1) * 8 * W] = transposed(both.astype(F32))
-
     centre_two, scale_two = scale_of(*join_stats(1, 1, stats, True))
 
     def gradient(grad, normed):
@@ -387,7 +412,8 @@
         first, second = sums
         for r in range(1, R + 1):
             normed = (h_ext[t + 2, r * W : (r + 1) * W, :].astype(F32) - centre_two) * scale_two
-            grad = gradient(t2_ext[t, r * W : (r + 1) * W, :], normed)
+            grad = gradient(t2[t, (r - 1) * W : r * W, :], normed)
+            t2[t, (r - 1) * W : r * W, :] = grad
             first = first + jnp.sum(grad, axis=0, keepdims=True)
             second = second + jnp.sum(grad * normed, axis=0, keepdims=True)
         return first, second
@@ -407,10 +433,12 @@
     put_stats(2, 1, *join_stats(2, 0, stats, False))
     stats = send_stats(2, 1)
 
-    @pl.loop(0, T)
-    def _(t):
-        block = v_ext[t + 2, W : (R + 1) * W, :].astype(F32) + conv(win_second, w_second, t, dot_turned)
+    def add_input(t, value, _):
+        block = v_ext[t + 2, W : (R + 1) * W, :].astype(F32) + value
         b_ext[t + 2, W : (R + 1) * W, :] = block.astype(BF16)
+
+    conv(win_second, w_second, wide, dot_turned)
+    frames_of(add_input, None)
 
     block_halo = begins([
         halo(17, b_ext.at[T : T + 2, own], b_ext.at[0:2, own], near(1, False)),
@@ -490,18 +518,18 @@
             value = self.full[self.part(plane), :]
             for k in range(PLANE - 1):
                 value = value + self.recv[k].astype(F32)
-            self.sums[...] = value
+            self.sums[...] = value.astype(BF16)
             self.copies = begins([
                 remote(self.sums, self.recvb.at[column], *self.sem(wb_sems, k), column_peer(k))
                 for k in range(1, COLUMN)
             ])
-            self.recvb[column] = value
+            self.recvb[column] = value.astype(BF16)
 
         def third(self):
             ends(self.copies)
-            value = self.recvb[0]
+            value = self.recvb[0].astype(F32)
             for k in range(1, COLUMN):
-                value = value + self.recvb[k]
+                value = value + self.recvb[k].astype(F32)
             value = value * (1.0 / math.sqrt(2 * 128 * 8 * 160))
             here = self.part(plane)
             self.whole[here, :] = value.astype(BF16)
@@ -518,33 +546,48 @@
     sums_sd.start()
 
     count = 1.0 / (4 * GROUP_CELLS)
-    ends(act_halo)
     first, second = join_stats(2, 1, stats, False)
     mean_one, mean_two = over_group(first) * count, over_group(second) * count
 
-    @pl.loop(0, T + 2)
+    def hidden_row(f, r, normed, grad, mask):
+        hidden = scale_two * (grad - mean_one - normed * mean_two)
+        put_windows(win_back, f, r, hidden * mask)
+        return hidden
+
+    def second_normed(f, r):
+        return (h_ext[f + 2, r * W : (r + 1) * W, :].astype(F32) - centre_two) * scale_two
+
+    def far_row(f, r, mask):
+        normed = second_normed(f, r)
+        grad = gradient(t2_ext[f, r * W : (r + 1) * W, :].astype(F32), normed)
+        hidden_row(f, r, normed, grad, mask)
+
+    @pl.loop(0, T)
     def _(f):
-        late = jnp.where(f >= T, has_next, one)
-        for r in range(R + 2):
-            normed = (h_ext[f + 2, r * W : (r + 1) * W, :].astype(F32) - centre_two) * scale_two
-            grad = gradient(t2_ext[f, r * W : (r + 1) * W, :], normed)
-            hidden = scale_two * (grad - mean_one - normed * mean_two)
-            put_windows(win_back, f, r, hidden * (late * row_mask(r)))
-            if 1 <= r <= R:
-
-                @pl.when(f < T)
-                def _():
-                    field[f, (r - 1) * W : r * W, :] = hidden
+        for r in range(1, R + 1):
+            here = slice((r - 1) * W, r * W)
+            field[f, here, :] = hidden_row(f, r, second_normed(f, r), t2[f, here, :], one)
 
     for half in range(2):
         both = field[2 * half : 2 * half + 2].reshape(8 * W, L)
         gt[:, half * 8 * W : (half + 1) * 8 * W] = transposed(both)
     block_weights(win_first, full_f)
     sums_f.start()
+    ends(act_halo)
+
+    @pl.loop(0, T)
+    def _(f):
+        for r in (0, R + 1):
+            far_row(f, r, row_mask(r))
+
+    @pl.loop(T, T + 2)
+    def _(f):
+        for r in range(R + 2):
+            far_row(f, r, has_next * row_mask(r))
+
     sums_sd.second()
 
-    def back_first(t, sums):
-        back = conv(win_back, b_first, t, dot)
+    def back_first(t, back, sums):
         normed = (v_ext[t + 2, W : (R + 1) * W, :].astype(F32) - centre_one) * scale_one
         grad = gradient(back, normed)
         t1[t] = grad
@@ -553,7 +596,8 @@
             sums[1] + jnp.sum(grad * normed, axis=0, keepdims=True),
         )
 
-    put_stats(3, 0, *lax.fori_loop(0, T, back_first, nothing))
+    conv(win_back, b_first, wide, dot)
+    put_stats(3, 0, *frames_of(back_first, nothing))
     stats = send_stats(3, 0)
     sums_f.second()
 
@@ -610,8 +654,8 @@
             pltpu.VMEM((piece * PLANE, L), F32),
             pltpu.VMEM((piece * PLANE, L), BF16),
             pltpu.VMEM((PLANE - 1, piece, L), BF16),
-            pltpu.VMEM((piece, L), F32),
-            pltpu.VMEM((COLUMN, piece, L), F32),
+            pltpu.VMEM((piece, L), BF16),
+            pltpu.VMEM((COLUMN, piece, L), BF16),
         ]
 
     vmem = pl.BlockSpec(memory_space=pltpu.VMEM)
@@ -628,20 +672,21 @@
         out_specs=(vmem,) * 4,
         scratch_shapes=[
             pltpu.VMEM((C, TILES * L), F32),
-            pltpu.VMEM((9, 2 * C, 4 * C), BF16),
-            pltpu.VMEM((9, 2 * C, 4 * C), BF16),
-            pltpu.VMEM((9, 4 * C, 2 * C), BF16),
-            pltpu.VMEM((9, 4 * C, 2 * C), BF16),
+            pltpu.VMEM((4, 3, 4 * C, 4 * C), BF16),
+            pltpu.VMEM((4, 3, 4 * C, 4 * C), BF16),
+            pltpu.VMEM((4, 3, 4 * C, 4 * C), BF16),
+            pltpu.VMEM((4, 3, 4 * C, 4 * C), BF16),
             pltpu.VMEM((9, 2 * C, 2 * C_OUT), BF16),
+            pltpu.VMEM((T // 2 * R * W, 2 * L), F32),
             pltpu.VMEM((T + 2, rows, L), BF16),
             pltpu.VMEM((T, R * W, L), F32),
-            pltpu.VMEM((T + 2, 3 * W, L), BF16),
+            pltpu.VMEM((2 * T, 4 * W, L), BF16),
             pltpu.VMEM((T, 2 * W, L), F32),
-            pltpu.VMEM((T + 2, 3 * W, 2 * L), BF16),
+            pltpu.VMEM((2 * T, 4 * W, 2 * L), BF16),
             pltpu.VMEM((T, R * W, L), F32),
+            pltpu.VMEM((T + 4, rows, L), BF16),
             pltpu.VMEM((T + 2, rows, L), BF16),
-            pltpu.VMEM((T + 4, rows, L), BF16),
-            pltpu.VMEM((T + 2, rows, L), F32),
+            pltpu.VMEM((T, R * W, L), F32),
             pltpu.VMEM((T, R * W, L), F32),
             pltpu.VMEM((T + 2, rows, 2 * L), BF16),
             pltpu.VMEM((T + 2, rows, 2 * L), BF16),
@@ -694,7 +739,7 @@
         out_specs=(
             out_frame(2), out_frame(R), whole(C, 27 * C), whole(C, 27 * C), whole(27 * C, C_OUT)
         ),
-        compiler_params=pltpu.CompilerParams(vmem_limit_bytes=32 * 1024 * 1024),
+        compiler_params=pltpu.CompilerParams(vmem_limit_bytes=60 * 1024 * 1024),
     )(*results)
     return down, grad_video, first.T, second.T, grad_down
 

time: 94.4 us -> 89.3 us (0.946)
  the two profiles are of different devices: /device:TPU:65 before, /device:TPU:16 now
where the time goes in v3:
time: 89.3 us; the launch traced here: 89.1 us
  Pallas kernels  88.4 us (99%)
    pallas_call x1, Pallas kernels, local(): pl.pallas_call(kernel, out_shape=(jax.ShapeDtypeStruct((T, 2 * W, L), F32...  83.9 us
    pallas_call x1, Pallas kernels, local(): pl.pallas_call(finish_kernel, grid=(T,), out_shape=(jax.ShapeDtypeStruct(...  4.6 us

profile of v3, /device:TPU:16, one launch (start us, length us, event | category | flops | bytes accessed | tf_op | source)
XLA Modules:
  0.0 89.1 jit_solution(14374380472268842543)
XLA Ops:
  0.6 83.9 %shard_map.92 = (f32[4,160,128]{2,1,0:T(8,128)}, f32[4,320,128]{2,1,0:T(8,128)}, bf16[2816,128]{1,0:T(8,128)(2,1)}, bf16[1024,128]{1,0:T(8,128)(2,1)}) custom-call(bf16[1,4,4,10240]{3,2,1,0:T(4,128)(2,1)} %video.1, bf16[1,4,2,10240]{3,2,1,0:T(2,128)(2,1)} %cot.1, bf16[64,1728]{1,0:T(8,128)(2,1)} %bitcast.6, bf16[64,1728]{1,0:T(8,128)(2,1)} %bitcast.7, ...), custom_call_target="tpu_custom_call" | custom-call | tf_op jit(solution)/shard_map/pallas_call | solution.py:663
  84.5 4.6 %shard_map.93 = (bf16[1,4,2,10240]{3,2,1,0:T(2,128)(2,1)}, f32[1,4,4,10240]{3,2,1,0:T(4,128)}, f32[64,1728]{1,0:T(8,128)}, f32[64,1728]{1,0:T(8,128)}, f32[1728,128]{1,0:T(8,128)}) custom-call(f32[4,160,128]{2,1,0:T(8,128)} %get-tuple-element.14.down, f32[4,320,128]{2,1,0:T(8,128)} %get-tuple-element.15.video, bf16[2816,128]{1,0:T(8,128)(2,1)} %get-tuple-element.16.sums_sd, ...), custom_call_target="tpu_custom_call" | custom-call | tf_op jit(solution)/shard_map/pallas_call | solution.py:723

commit v4 on v3

--- a/solution.py
+++ b/solution.py
@@ -23,7 +23,8 @@
 HIGH = 8
 PLANE = 16
 COLUMN = 8
-PIECE_SD = 176
+PIECE_S = 64
+PIECE_D = 128
 PIECE_F = 64
 TILES = 14
 HALF = TILES * C
@@ -174,18 +175,20 @@
 
 def kernel(
     video, cot, raw_first, raw_second, w_down,
-    out_down, out_video, all_sd, all_f,
+    out_down, out_video, all_s, all_d, all_f,
     padded, w_first, w_second, b_first, b_second, b_down, wide,
     v_ext, field, c_ext, c_field, c_win, g_block, h_ext, t2_ext, t2, t1, win_first, win_second,
     win_back, b_ext, b_even, b_odd, gt, gtc, st_src, st_buf,
-    full_sd, send_sd, recv_sd, sum_sd, recvb_sd,
+    full_s, send_s, recv_s, sum_s, recvb_s,
+    full_d, send_d, recv_d, sum_d, recvb_d,
     full_f, send_f, recv_f, sum_f, recvb_f,
-    halo_sems, st_sems, wa_sems, wb_sems, wc_sems,
+    halo_sems, st_sems, wa_sems, wb_sems, wc_sems, wd_sems,
 ):
     tm, space = lax.axis_index("tm"), lax.axis_index("space")
     low = lax.rem(tm, LOW)
     high = (tm // LOW) * 2 + space
     plane, column = plane_place(), column_place()
+    core = lax.rem(tm, 2)
     has_past = jnp.where(tm == 0, 0.0, 1.0).astype(F32)
     has_next = jnp.where(tm == TM - 1, 0.0, 1.0).astype(F32)
     has_above = jnp.where(space == 0, 0.0, 1.0).astype(F32)
@@ -446,6 +449,66 @@
         halo(19, b_ext.at[T : T + 2, pl.ds(R * W, W)], b_ext.at[0:2, pl.ds(0, W)], near(1, True)),
     ])
 
+    class Reduction:
+        def __init__(self, number, piece, full, send, recv, sums, recvb, whole):
+            self.n, self.half = number, piece // 2
+            self.full, self.send, self.recv, self.sums = full, send, recv, sums
+            self.recvb, self.whole = recvb, whole
+
+        def sem(self, sems, *k):
+            return sems.at[(0, self.n) + k], sems.at[(1, self.n) + k]
+
+        def start(self):
+            self.send[...] = self.full[...].reshape(self.send.shape).astype(BF16)
+            self.copies = begins([
+                remote(
+                    self.send.at[:, lax.rem(plane + k, PLANE)], self.recv.at[k - 1],
+                    *self.sem(wa_sems, k), plane_peer(k),
+                )
+                for k in range(1, PLANE)
+            ])
+
+        def second(self):
+            ends(self.copies)
+            for h in range(2):
+                row = pl.multiple_of((h * PLANE + plane) * self.half, 16)
+                value = self.full[pl.ds(row, self.half), :]
+                for k in range(PLANE - 1):
+                    value = value + self.recv[k, h].astype(F32)
+                self.sums[h] = value.astype(BF16)
+            self.copies = begins([
+                remote(
+                    self.sums.at[lax.rem(column + k, COLUMN) // 4], self.recvb.at[column],
+                    *self.sem(wb_sems, k), column_peer(k),
+                )
+                for k in range(1, COLUMN)
+            ])
+            self.recvb[column] = self.sums[core]
+
+        def third(self):
+            ends(self.copies)
+            value = self.recvb[0].astype(F32)
+            for k in range(1, COLUMN):
+                value = value + self.recvb[k].astype(F32)
+            value = value * (1.0 / math.sqrt(2 * 128 * 8 * 160))
+            self.whole[core, plane] = value.astype(BF16)
+            here = self.whole.at[core, plane]
+            self.copies = begins([
+                remote(here, here, *self.sem(wc_sems, k), plane_peer(k)) for k in range(1, PLANE)
+            ])
+
+        def fourth(self):
+            ends(self.copies)
+            here = self.whole.at[core]
+            self.copies = begins([remote(here, here, *self.sem(wd_sems), {"tm": tm + 1 - 2 * core})])
+
+        def finish(self):
+            ends(self.copies)
+
+    sums_s = Reduction(0, PIECE_S, full_s, send_s, recv_s, sum_s, recvb_s, all_s)
+    sums_d = Reduction(1, PIECE_D, full_d, send_d, recv_d, sum_d, recvb_d, all_d)
+    sums_f = Reduction(2, PIECE_F, full_f, send_f, recv_f, sum_f, recvb_f, all_f)
+
     def block_weights(windows, full):
         left = lanes((C, L)) < C
 
@@ -467,9 +530,11 @@
         put(12, value[:, 0:L])
         put(13, jnp.where(left, value[:, L : 2 * L], 0.0))
 
-    full_sd[HALF + 27 * C :, :] = jnp.zeros((full_sd.shape[0] - HALF - 27 * C, L), F32)
+    full_s[HALF:, :] = jnp.zeros((full_s.shape[0] - HALF, L), F32)
+    full_d[27 * C :, :] = jnp.zeros((full_d.shape[0] - 27 * C, L), F32)
     full_f[HALF:, :] = jnp.zeros((full_f.shape[0] - HALF, L), F32)
-    block_weights(win_second, full_sd)
+    block_weights(win_second, full_s)
+    sums_s.start()
 
     ends(block_halo)
 
@@ -488,62 +553,10 @@
             ref, start = projected(dr)
             cells = ref[dt : dt + T, start : start + 2 * W, :].reshape(2 * W * T, 2 * L)
             turned = jnp.dot(gtc[...], cells, preferred_element_type=F32).T
-            base = HALF + (dt * 3 + dr) * 3 * C
-            full_sd[base : base + 3 * C, :] = turned[0 : 3 * C]
-
-    class Reduction:
-        def __init__(self, number, piece, full, send, recv, sums, recvb, whole):
-            self.n, self.piece = number, piece
-            self.full, self.send, self.recv, self.sums = full, send, recv, sums
-            self.recvb, self.whole = recvb, whole
-
-        def sem(self, sems, k):
-            return sems.at[0, self.n, k], sems.at[1, self.n, k]
-
-        def part(self, index):
-            return pl.ds(pl.multiple_of(index * self.piece, 16), self.piece)
-
-        def start(self):
-            self.send[...] = self.full[...].astype(BF16)
-            self.copies = begins([
-                remote(
-                    self.send.at[self.part(lax.rem(plane + k, PLANE))], self.recv.at[k - 1],
-                    *self.sem(wa_sems, k), plane_peer(k),
-                )
-                for k in range(1, PLANE)
-            ])
-
-        def second(self):
-            ends(self.copies)
-            value = self.full[self.part(plane), :]
-            for k in range(PLANE - 1):
-                value = value + self.recv[k].astype(F32)
-            self.sums[...] = value.astype(BF16)
-            self.copies = begins([
-                remote(self.sums, self.recvb.at[column], *self.sem(wb_sems, k), column_peer(k))
-                for k in range(1, COLUMN)
-            ])
-            self.recvb[column] = value.astype(BF16)
-
-        def third(self):
-            ends(self.copies)
-            value = self.recvb[0].astype(F32)
-            for k in range(1, COLUMN):
-                value = value + self.recvb[k].astype(F32)
-            value = value * (1.0 / math.sqrt(2 * 128 * 8 * 160))
-            here = self.part(plane)
-            self.whole[here, :] = value.astype(BF16)
-            self.copies = begins([
-                remote(self.whole.at[here], self.whole.at[here], *self.sem(wc_sems, k), plane_peer(k))
-                for k in range(1, PLANE)
-            ])
-
-        def finish(self):
-            ends(self.copies)
-
-    sums_sd = Reduction(0, PIECE_SD, full_sd, send_sd, recv_sd, sum_sd, recvb_sd, all_sd)
-    sums_f = Reduction(1, PIECE_F, full_f, send_f, recv_f, sum_f, recvb_f, all_f)
-    sums_sd.start()
+            base = (dt * 3 + dr) * 3 * C
+            full_d[base : base + 3 * C, :] = turned[0 : 3 * C]
+    sums_d.start()
+
 
     count = 1.0 / (4 * GROUP_CELLS)
     first, second = join_stats(2, 1, stats, False)
@@ -573,6 +586,7 @@
         gt[:, half * 8 * W : (half + 1) * 8 * W] = transposed(both)
     block_weights(win_first, full_f)
     sums_f.start()
+    sums_s.second()
     ends(act_halo)
 
     @pl.loop(0, T)
@@ -585,7 +599,7 @@
         for r in range(R + 2):
             far_row(f, r, has_next * row_mask(r))
 
-    sums_sd.second()
+    sums_d.second()
 
     def back_first(t, back, sums):
         normed = (v_ext[t + 2, W : (R + 1) * W, :].astype(F32) - centre_one) * scale_one
@@ -599,6 +613,7 @@
     conv(win_back, b_first, wide, dot)
     put_stats(3, 0, *frames_of(back_first, nothing))
     stats = send_stats(3, 0)
+    sums_s.third()
     sums_f.second()
 
     @pl.loop(0, T)
@@ -611,9 +626,9 @@
                 total = part if total is None else total + part
         out_down[t] = total
 
+    sums_d.third()
     put_stats(3, 1, *join_stats(3, 0, stats, False))
     stats = send_stats(3, 1)
-    sums_sd.third()
     sums_f.third()
     first, second = join_stats(3, 1, stats, False)
     mean_one, mean_two = over_group(first) * count, over_group(second) * count
@@ -623,24 +638,23 @@
         normed = (v_ext[t + 2, W : (R + 1) * W, :].astype(F32) - centre_one) * scale_one
         out_video[t] = g_block[t] + scale_one * (t1[t] - mean_one - normed * mean_two)
 
-    sums_sd.finish()
-    sums_f.finish()
-
-
-def finish_kernel(down, video, sums_sd, sums_f, out_down, out_video, out_first, out_second, out_grad_down):
+    for sums in (sums_s, sums_d, sums_f):
+        sums.fourth()
+    for sums in (sums_s, sums_d, sums_f):
+        sums.finish()
+
+
+def finish_kernel(down, video, sums_s, sums_d, sums_f, out_down, out_video, out_first, out_second, out_grad_down):
     for p in range(W):
         here = slice(p * L, (p + 1) * L)
         out_video[0, 0, :, here] = video[0, pl.ds(p, R, stride=W), :]
         out_down[0, 0, :, here] = down[0, pl.ds(p, 2, stride=W), :].astype(BF16)
 
-    @pl.when(pl.program_id(0) == 0)
-    def _():
-        for source, target in ((sums_sd, out_second), (sums_f, out_first)):
-            for tile in range(TILES):
-                width = min(L, 27 * C - tile * L)
-                value = source[tile * C : (tile + 1) * C, :].astype(F32)
-                target[:, tile * L : tile * L + width] = value[:, 0:width]
-        out_grad_down[...] = sums_sd[HALF : HALF + 27 * C, :].astype(F32)
+    for source, target in ((sums_s, out_second), (sums_f, out_first)):
+        for tile in range(PLANE // T):
+            value = source[tile * C : (tile + 1) * C, :].astype(F32)
+            target[:, tile * L : (tile + 1) * L] = value
+    out_grad_down[...] = sums_d[...].astype(F32)
 
 
 def local(video, conv_first, conv_second, conv_down, down_cotangent):
@@ -650,12 +664,13 @@
     rows = (R + 2) * W
 
     def reduction(piece):
+        half = (2, piece // 2, L)
         return [
             pltpu.VMEM((piece * PLANE, L), F32),
-            pltpu.VMEM((piece * PLANE, L), BF16),
-            pltpu.VMEM((PLANE - 1, piece, L), BF16),
-            pltpu.VMEM((piece, L), BF16),
-            pltpu.VMEM((COLUMN, piece, L), BF16),
+            pltpu.VMEM((2, PLANE, piece // 2, L), BF16),
+            pltpu.VMEM((PLANE - 1,) + half, BF16),
+            pltpu.VMEM(half, BF16),
+            pltpu.VMEM((COLUMN,) + half[1:], BF16),
         ]
 
     vmem = pl.BlockSpec(memory_space=pltpu.VMEM)
@@ -665,11 +680,13 @@
         out_shape=(
             jax.ShapeDtypeStruct((T, 2 * W, L), F32),
             jax.ShapeDtypeStruct((T, R * W, L), F32),
-            jax.ShapeDtypeStruct((PIECE_SD * PLANE, L), BF16),
-            jax.ShapeDtypeStruct((PIECE_F * PLANE, L), BF16),
+            *(
+                jax.ShapeDtypeStruct((2, PLANE, piece // 2, L), BF16)
+                for piece in (PIECE_S, PIECE_D, PIECE_F)
+            ),
         ),
         in_specs=[vmem] * len(operands),
-        out_specs=(vmem,) * 4,
+        out_specs=(vmem,) * 5,
         scratch_shapes=[
             pltpu.VMEM((C, TILES * L), F32),
             pltpu.VMEM((4, 3, 4 * C, 4 * C), BF16),
@@ -698,13 +715,15 @@
             pltpu.VMEM((L, CELLS // 2), BF16),
             pltpu.VMEM((4, 2, 8, L), F32),
             pltpu.VMEM((4, 2, LOW, 8, L), F32),
-            *reduction(PIECE_SD),
+            *reduction(PIECE_S),
+            *reduction(PIECE_D),
             *reduction(PIECE_F),
             dma((2, 20)),
             dma((2, 4, 2, LOW)),
-            dma((2, 2, PLANE)),
-            dma((2, 2, COLUMN)),
-            dma((2, 2, PLANE)),
+            dma((2, 3, PLANE)),
+            dma((2, 3, COLUMN)),
+            dma((2, 3, PLANE)),
+            dma((2, 3)),
         ],
         compiler_params=pltpu.CompilerParams(
             collective_id=1, has_side_effects=True, vmem_limit_bytes=56 * 1024 * 1024
@@ -716,9 +735,6 @@
 
     def out_frame(rows):
         return pl.BlockSpec((1, 1, rows, W * L), lambda t: (0, t, 0, 0))
-
-    def whole(*shape):
-        return pl.BlockSpec(shape, lambda t: (0,) * len(shape))
 
     down, grad_video, first, second, grad_down = pl.pallas_call(
         finish_kernel,
@@ -733,14 +749,19 @@
         in_specs=[
             frame(1, 2 * W, L),
             frame(1, R * W, L),
-            whole(PIECE_SD * PLANE, L),
-            whole(PIECE_F * PLANE, L),
+            frame(PIECE_S * PLANE // T, L),
+            frame(27 * C // T, L),
+            frame(PIECE_F * PLANE // T, L),
         ],
         out_specs=(
-            out_frame(2), out_frame(R), whole(C, 27 * C), whole(C, 27 * C), whole(27 * C, C_OUT)
+            out_frame(2),
+            out_frame(R),
+            pl.BlockSpec((C, PLANE // T * L), lambda t: (0, t)),
+            pl.BlockSpec((C, PLANE // T * L), lambda t: (0, t)),
+            frame(27 * C // T, C_OUT),
         ),
         compiler_params=pltpu.CompilerParams(vmem_limit_bytes=60 * 1024 * 1024),
-    )(*results)
+    )(*results[:2], *(sums.reshape(-1, L) for sums in results[2:]))
     return down, grad_video, first.T, second.T, grad_down
 
 

time: 89.3 us -> 81.8 us (0.916)
  the two profiles are of different devices: /device:TPU:16 before, /device:TPU:1 now
where the time goes in v4:
time: 81.8 us; the launch traced here: 81.5 us
  Pallas kernels  80.9 us (99%)
    pallas_call x1, Pallas kernels, local(): pl.pallas_call(kernel, out_shape=(jax.ShapeDtypeStruct((T, 2 * W, L), F32...  76.9 us
    pallas_call x1, Pallas kernels, local(): pl.pallas_call(finish_kernel, grid=(T,), out_shape=(jax.ShapeDtypeStruct(...  3.99 us

profile of v4, /device:TPU:1, one launch (start us, length us, event | category | flops | bytes accessed | tf_op | source)
XLA Modules:
  0.0 81.5 jit_solution(15817015385168061895)
XLA Ops:
  0.6 76.9 %shard_map.92 = (f32[4,160,128]{2,1,0:T(8,128)}, f32[4,320,128]{2,1,0:T(8,128)}, bf16[2,16,32,128]{3,2,1,0:T(8,128)(2,1)}, bf16[2,16,64,128]{3,2,1,0:T(8,128)(2,1)}, bf16[2,16,32,128]{3,2,1,0:T(8,128)(2,1)}) custom-call(bf16[1,4,4,10240]{3,2,1,0:T(4,128)(2,1)} %video.1, bf16[1,4,2,10240]{3,2,1,0:T(2,128)(2,1)} %cot.1, bf16[64,1728]{1,0:T(8,128)(2,1)} %bitcast.12, ...), custom_call_target="tpu_custom_call" | custom-call | tf_op jit(solution)/shard_map/pallas_call | solution.py:678
  77.6 4.0 %shard_map.93 = (bf16[1,4,2,10240]{3,2,1,0:T(2,128)(2,1)}, f32[1,4,4,10240]{3,2,1,0:T(4,128)}, f32[64,1728]{1,0:T(8,128)}, f32[64,1728]{1,0:T(8,128)}, f32[1728,128]{1,0:T(8,128)}) custom-call(f32[4,160,128]{2,1,0:T(8,128)} %get-tuple-element.15.down, f32[4,320,128]{2,1,0:T(8,128)} %get-tuple-element.16.video, bf16[1024,128]{1,0:T(8,128)(2,1)} %bitcast.10, ...), custom_call_target="tpu_custom_call" | custom-call | tf_op jit(solution)/shard_map/pallas_call | solution.py:739

commit v5 on v4

--- a/solution.py
+++ b/solution.py
@@ -611,10 +611,10 @@
         )
 
     conv(win_back, b_first, wide, dot)
+    sums_f.second()
     put_stats(3, 0, *frames_of(back_first, nothing))
     stats = send_stats(3, 0)
     sums_s.third()
-    sums_f.second()
 
     @pl.loop(0, T)
     def _(t):

time: 81.8 us -> 81.9 us (level)
  no operation moved by 1% of the time
where the time goes in v5:
time: 81.9 us; the launch traced here: 81.7 us
  Pallas kernels  81 us (99%)
    pallas_call x1, Pallas kernels, local(): pl.pallas_call(kernel, out_shape=(jax.ShapeDtypeStruct((T, 2 * W, L), F32...  77.1 us
    pallas_call x1, Pallas kernels, local(): pl.pallas_call(finish_kernel, grid=(T,), out_shape=(jax.ShapeDtypeStruct(...  3.99 us

profile of v5, /device:TPU:1, one launch (start us, length us, event | category | flops | bytes accessed | tf_op | source)
XLA Modules:
  0.0 81.7 jit_solution(6314187242664340065)
XLA Ops:
  0.6 77.1 %shard_map.92 = (f32[4,160,128]{2,1,0:T(8,128)}, f32[4,320,128]{2,1,0:T(8,128)}, bf16[2,16,32,128]{3,2,1,0:T(8,128)(2,1)}, bf16[2,16,64,128]{3,2,1,0:T(8,128)(2,1)}, bf16[2,16,32,128]{3,2,1,0:T(8,128)(2,1)}) custom-call(bf16[1,4,4,10240]{3,2,1,0:T(4,128)(2,1)} %video.1, bf16[1,4,2,10240]{3,2,1,0:T(2,128)(2,1)} %cot.1, bf16[64,1728]{1,0:T(8,128)(2,1)} %bitcast.12, ...), custom_call_target="tpu_custom_call" | custom-call | tf_op jit(solution)/shard_map/pallas_call | solution.py:678
  77.7 4.0 %shard_map.93 = (bf16[1,4,2,10240]{3,2,1,0:T(2,128)(2,1)}, f32[1,4,4,10240]{3,2,1,0:T(4,128)}, f32[64,1728]{1,0:T(8,128)}, f32[64,1728]{1,0:T(8,128)}, f32[1728,128]{1,0:T(8,128)}) custom-call(f32[4,160,128]{2,1,0:T(8,128)} %get-tuple-element.15.down, f32[4,320,128]{2,1,0:T(8,128)} %get-tuple-element.16.video, bf16[1024,128]{1,0:T(8,128)(2,1)} %bitcast.10, ...), custom_call_target="tpu_custom_call" | custom-call | tf_op jit(solution)/shard_map/pallas_call | solution.py:739
